TPU v7x, 32 devices: a whole 2x2x4 slice. The times are simulated.
32 devices in a mesh: frames: 8 (over y, x, core), chan: 4 (over z).
Axes of the slice: x: 2, y: 2, z: 4, core: 2. Of those that a mesh axis runs over, the one named last changes fastest.
Arguments:
- fields: bfloat16 [8, 3, 72, 64, 1536], P('frames', None, 'chan'), may hold values from -6 to 6
- lead_index: int32 [8], P('frames'), may hold values from 0 to 39
- embed_weight: bfloat16 [3, 72, 64, 768], P(None, 'chan'), may hold values from -0.0546875 to 0.0546875
- position_embed: bfloat16 [1536, 768], P('chan'), may hold values from -3 to 3
- lead_table: bfloat16 [40, 768], replicated, may hold values from -3 to 3
- attend_gain: float32 [768], replicated, may hold values from 0.5 to 1.5
- attend_shift: float32 [768], replicated, may hold values from -1.2 to 1.2
- attend_weight: bfloat16 [768, 2304], replicated, may hold values from -0.21875 to 0.21875
- out_weight: bfloat16 [768, 768], replicated, may hold values from -0.875 to 0.875
- out_bias: float32 [768], replicated, may hold values from -1.2 to 1.2
- mixer_gain: float32 [768], replicated, may hold values from 0.5 to 1.5
- mixer_shift: float32 [768], replicated, may hold values from -1.2 to 1.2
- up_weight: bfloat16 [768, 3072], replicated, may hold values from -0.21875 to 0.21875
- up_bias: float32 [3072], replicated, may hold values from -1.2 to 1.2
- down_weight: bfloat16 [3072, 768], replicated, may hold values from -0.109375 to 0.109375
- down_bias: float32 [768], replicated, may hold values from -1.2 to 1.2
- head_weight: bfloat16 [768, 192], replicated, may hold values from -0.109375 to 0.109375
- specialist_cell_offset: float32 [3, 72, 64], P(None, 'chan'), may hold values from -3 to 3
- cotangent: bfloat16 [8, 72, 64, 1536], P('frames', 'chan'), may hold values from -6 to 6
Outputs:
- mixed_prediction: bfloat16 [8, 72, 64, 1536], P('frames', 'chan')
- fields_grad: bfloat16 [8, 3, 72, 64, 1536], P('frames', None, 'chan')
- embed_grad: float32 [3, 72, 64, 768], P(None, 'chan', None, 'frames')
- position_grad: float32 [1536, 768], P('chan', 'frames')
- table_grad: float32 [40, 768], P(None, ('frames', 'chan'))
- attend_gain_grad: float32 [768], P(('frames', 'chan'))
- attend_shift_grad: float32 [768], P(('frames', 'chan'))
- attend_weight_grad: float32 [768, 2304], P(('frames', 'chan'))
- out_weight_grad: float32 [768, 768], P(('frames', 'chan'))
- out_bias_grad: float32 [768], P(('frames', 'chan'))
- mixer_gain_grad: float32 [768], P(('frames', 'chan'))
- mixer_shift_grad: float32 [768], P(('frames', 'chan'))
- up_weight_grad: float32 [768, 3072], P(('frames', 'chan'))
- up_bias_grad: float32 [3072], P(('frames', 'chan'))
- down_weight_grad: float32 [3072, 768], P(('frames', 'chan'))
- down_bias_grad: float32 [768], P(('frames', 'chan'))
- head_weight_grad: float32 [768, 192], P(('frames', 'chan'))
- expert_bias_grad: float32 [3, 72, 64], P(None, 'chan', 'frames')
All inputs are finite; a program needn't handle non-finite values.
Results may differ from a plain program's by a relative error of at most 0.023.
Values may be sent and summed in bfloat16 or wider, within the bound.
No kernel may reach another device: no remote copies, remote signals or barrier semaphores. Data moves between devices by JAX's collectives and lax.ppermute only.
A program may use at most 320 MiB of HBM per device.

v0:
```python
from functools import partial

import jax
import jax.numpy as jnp
from jax import lax
from jax.sharding import PartitionSpec as P

HEADS = 12
HEAD_DIM = 64
EXP = 3
PIX = 64


epsilon = 1e-05


def layer_norm(v, gain, shift):
    average = jnp.mean(v, axis=-1, keepdims=True)
    centred = v - average
    spread = jnp.mean(centred * centred, axis=-1, keepdims=True)
    return centred * lax.rsqrt(spread + epsilon) * gain + shift


def tensor_dot_routine(left, right, left_dim, right_dim):
    return lax.dot_general(
        left, right, (((left_dim,), (right_dim,)), ((), ())), preferred_element_type=jnp.float32
    )


def on_device(
    fields,
    lead_index,
    embed_weight,
    position_embed,
    lead_table,
    attend_gain,
    attend_shift,
    attend_weight,
    out_weight,
    out_bias,
    mixer_gain,
    mixer_shift,
    up_weight,
    up_bias,
    down_weight,
    down_bias,
    head_weight,
    specialist_cell_offset,
    cotangent,
):
    model_width = attend_gain.shape[0]
    snapshot_source_variables = fields[0]
    reshaped_source_matrix = snapshot_source_variables.reshape(
        -1, snapshot_source_variables.shape[-1]
    )
    flattened_weight = embed_weight.reshape(-1, model_width)
    patches = reshaped_source_matrix.shape[1]
    rows_here = position_embed.shape[0]
    factor = HEAD_DIM ** (-0.5)
    embedded = lax.psum_scatter(
        tensor_dot_routine(reshaped_source_matrix, flattened_weight, 0, 0).astype(jnp.bfloat16),
        "chan",
        scatter_dimension=0,
        tiled=True,
    ).astype(jnp.float32)
    onehot = (
        lead_index[:, None] == jnp.arange(lead_table.shape[0], dtype=jnp.int32)[None, :]
    ).astype(jnp.bfloat16)
    lead_vector = tensor_dot_routine(onehot, lead_table, 1, 0)
    stream_start = embedded + position_embed.astype(jnp.float32) + lead_vector
    normed_first = layer_norm(stream_start, attend_gain, attend_shift).astype(jnp.bfloat16)
    packed = jnp.dot(normed_first, attend_weight, preferred_element_type=jnp.float32).astype(
        jnp.bfloat16
    )
    queries = packed[:, :model_width].reshape(rows_here, HEADS, HEAD_DIM)
    keys_values = lax.all_gather(packed[:, model_width:], "chan", axis=0, tiled=True)
    key_rows = keys_values[:, :model_width].reshape(patches, HEADS, HEAD_DIM)
    values = keys_values[:, model_width:].reshape(patches, HEADS, HEAD_DIM)
    scores = (
        jnp.einsum("qhd,khd->hqk", queries, key_rows, preferred_element_type=jnp.float32) * factor
    )
    log_total = jax.nn.logsumexp(scores, axis=-1, keepdims=True)
    shares = jnp.exp(scores - log_total)
    attended = (
        jnp.einsum(
            "hqk,khd->qhd", shares.astype(jnp.bfloat16), values, preferred_element_type=jnp.float32
        )
        .astype(jnp.bfloat16)
        .reshape(rows_here, model_width)
    )
    stream_mid = (
        stream_start + jnp.dot(attended, out_weight, preferred_element_type=jnp.float32) + out_bias
    )
    normed_second = layer_norm(stream_mid, mixer_gain, mixer_shift).astype(jnp.bfloat16)
    hidden = jnp.dot(normed_second, up_weight, preferred_element_type=jnp.float32) + up_bias
    active = jax.nn.gelu(hidden, approximate=True).astype(jnp.bfloat16)
    stream_end = (
        stream_mid + jnp.dot(active, down_weight, preferred_element_type=jnp.float32) + down_bias
    )
    end_low = stream_end.astype(jnp.bfloat16)
    logits_here = tensor_dot_routine(head_weight, end_low, 0, 1)
    logits_all = lax.all_gather(
        logits_here.astype(jnp.bfloat16), "chan", axis=1, tiled=True
    ).astype(logits_here.dtype)
    specialist_mixing_shares = jax.nn.softmax(logits_all.reshape(EXP, PIX, patches), axis=0)
    merged_prediction = (
        snapshot_source_variables.astype(jnp.float32) + specialist_cell_offset[:, :, :, None]
    )
    mixed_prediction = jnp.sum(specialist_mixing_shares[:, None] * merged_prediction, axis=0)
    output = mixed_prediction.astype(jnp.bfloat16)[None]
    incoming_cotangent = cotangent[0].astype(jnp.float32)
    merged_prediction_cotangent = specialist_mixing_shares[:, None] * incoming_cotangent[None]
    offset_sensitivity_share = jnp.sum(merged_prediction_cotangent, axis=3)
    mixing_share_cotangent = jnp.sum(merged_prediction * incoming_cotangent[None], axis=1)
    logit_part = specialist_mixing_shares * (
        mixing_share_cotangent
        - jnp.sum(specialist_mixing_shares * mixing_share_cotangent, axis=0, keepdims=True)
    )
    logit_low = lax.psum_scatter(
        logit_part.reshape(EXP * PIX, patches).astype(jnp.bfloat16),
        "chan",
        scatter_dimension=1,
        tiled=True,
    )
    head_grad = tensor_dot_routine(end_low, logit_low, 0, 1)
    stream_grad = tensor_dot_routine(logit_low, head_weight, 0, 1)
    down_bias_grad = jnp.sum(stream_grad, axis=0)
    down_low = stream_grad.astype(jnp.bfloat16)
    down_grad = tensor_dot_routine(active, down_low, 0, 0)
    active_grad = tensor_dot_routine(down_low, down_weight, 1, 1)
    gelu_pull = jax.vjp(partial(jax.nn.gelu, approximate=True), hidden)[1]
    hidden_grad = gelu_pull(active_grad)[0]
    up_bias_grad = jnp.sum(hidden_grad, axis=0)
    hidden_low = hidden_grad.astype(jnp.bfloat16)
    up_grad = tensor_dot_routine(normed_second, hidden_low, 0, 0)
    second_grad = tensor_dot_routine(hidden_low, up_weight, 1, 1)
    mixer_pull = jax.vjp(layer_norm, stream_mid, mixer_gain, mixer_shift)[1]
    mid_part, mixer_gain_grad, mixer_shift_grad = mixer_pull(second_grad)
    stream_grad = stream_grad + mid_part
    out_bias_grad = jnp.sum(stream_grad, axis=0)
    branch_low = stream_grad.astype(jnp.bfloat16)
    out_grad = tensor_dot_routine(attended, branch_low, 0, 0)
    attended_low = (
        tensor_dot_routine(branch_low, out_weight, 1, 1)
        .astype(jnp.bfloat16)
        .reshape(rows_here, HEADS, HEAD_DIM)
    )
    scores_again = (
        jnp.einsum("qhd,khd->hqk", queries, key_rows, preferred_element_type=jnp.float32) * factor
    )
    shares_again = jnp.exp(scores_again - log_total)
    share_grad = jnp.einsum(
        "qhd,khd->hqk", attended_low, values, preferred_element_type=jnp.float32
    )
    row_inner = jnp.sum(shares_again * share_grad, axis=-1, keepdims=True)
    score_low = (shares_again * (share_grad - row_inner)).astype(jnp.bfloat16)
    query_grad = (
        jnp.einsum("hqk,khd->qhd", score_low, key_rows, preferred_element_type=jnp.float32) * factor
    )
    key_part = (
        jnp.einsum("hqk,qhd->khd", score_low, queries, preferred_element_type=jnp.float32) * factor
    )
    value_part = jnp.einsum(
        "hqk,qhd->khd",
        shares_again.astype(jnp.bfloat16),
        attended_low,
        preferred_element_type=jnp.float32,
    )
    remote_part = jnp.concatenate(
        [key_part.reshape(patches, model_width), value_part.reshape(patches, model_width)], axis=1
    )
    remote_grad = lax.psum_scatter(
        remote_part.astype(jnp.bfloat16), "chan", scatter_dimension=0, tiled=True
    ).astype(jnp.float32)
    packed_low = jnp.concatenate(
        [query_grad.reshape(rows_here, model_width), remote_grad], axis=1
    ).astype(jnp.bfloat16)
    attend_grad = tensor_dot_routine(normed_first, packed_low, 0, 0)
    first_grad = tensor_dot_routine(packed_low, attend_weight, 1, 1)
    attend_pull = jax.vjp(layer_norm, stream_start, attend_gain, attend_shift)[1]
    start_part, attend_gain_grad, attend_shift_grad = attend_pull(first_grad)
    start_grad = stream_grad + start_part
    table_grad = jnp.transpose(onehot.astype(jnp.float32)) * jnp.sum(start_grad, axis=0)[None, :]
    start_low = start_grad.astype(jnp.bfloat16)
    start_outputs_every = lax.all_gather(start_low, "chan", axis=0, tiled=True)
    embed_part = tensor_dot_routine(reshaped_source_matrix, start_outputs_every, 1, 0).reshape(
        embed_weight.shape
    )
    source_cotangent = merged_prediction_cotangent.reshape(
        reshaped_source_matrix.shape
    ) + tensor_dot_routine(flattened_weight, start_outputs_every, 1, 1)
    fields_grad = source_cotangent.astype(jnp.bfloat16).reshape(fields.shape)
    embed_sum, position_sum, bias_sum = (
        lax.psum_scatter(
            embed_part.astype(jnp.bfloat16), "frames", scatter_dimension=3, tiled=True
        ).astype(jnp.float32),
        lax.psum_scatter(
            start_grad.astype(jnp.bfloat16), "frames", scatter_dimension=1, tiled=True
        ).astype(jnp.float32),
        lax.psum_scatter(
            offset_sensitivity_share.astype(jnp.bfloat16), "frames", scatter_dimension=2, tiled=True
        ).astype(jnp.float32),
    )
    (
        table_sum,
        attend_gain_sum,
        attend_shift_sum,
        attend_sum,
        out_sum,
        out_bias_sum,
        mixer_gain_sum,
        mixer_shift_sum,
        up_sum,
        up_bias_sum,
        down_sum,
        down_bias_sum,
        head_sum,
    ) = (
        lax.psum_scatter(table_grad, ("frames", "chan"), scatter_dimension=1, tiled=True),
        lax.psum_scatter(attend_gain_grad, ("frames", "chan"), scatter_dimension=0, tiled=True),
        lax.psum_scatter(attend_shift_grad, ("frames", "chan"), scatter_dimension=0, tiled=True),
        lax.psum_scatter(attend_grad, ("frames", "chan"), scatter_dimension=0, tiled=True),
        lax.psum_scatter(out_grad, ("frames", "chan"), scatter_dimension=0, tiled=True),
        lax.psum_scatter(out_bias_grad, ("frames", "chan"), scatter_dimension=0, tiled=True),
        lax.psum_scatter(mixer_gain_grad, ("frames", "chan"), scatter_dimension=0, tiled=True),
        lax.psum_scatter(mixer_shift_grad, ("frames", "chan"), scatter_dimension=0, tiled=True),
        lax.psum_scatter(up_grad, ("frames", "chan"), scatter_dimension=0, tiled=True),
        lax.psum_scatter(up_bias_grad, ("frames", "chan"), scatter_dimension=0, tiled=True),
        lax.psum_scatter(down_grad, ("frames", "chan"), scatter_dimension=0, tiled=True),
        lax.psum_scatter(down_bias_grad, ("frames", "chan"), scatter_dimension=0, tiled=True),
        lax.psum_scatter(head_grad, ("frames", "chan"), scatter_dimension=0, tiled=True),
    )
    return (
        output,
        fields_grad,
        embed_sum,
        position_sum,
        table_sum,
        attend_gain_sum,
        attend_shift_sum,
        attend_sum,
        out_sum,
        out_bias_sum,
        mixer_gain_sum,
        mixer_shift_sum,
        up_sum,
        up_bias_sum,
        down_sum,
        down_bias_sum,
        head_sum,
        bias_sum,
    )


def solution(mesh):
    in_specs = (
        P("frames", None, "chan", None, None),
        P("frames"),
        P(None, "chan", None, None),
        P("chan", None),
        P(),
        P(),
        P(),
        P(),
        P(),
        P(),
        P(),
        P(),
        P(),
        P(),
        P(),
        P(),
        P(),
        P(None, "chan", None),
        P("frames", "chan", None, None),
    )
    out_specs = (
        P("frames", "chan", None, None),
        P("frames", None, "chan", None, None),
        P(None, "chan", None, "frames"),
        P("chan", "frames"),
        P(None, ("frames", "chan")),
        P(("frames", "chan")),
        P(("frames", "chan")),
        P(("frames", "chan"), None),
        P(("frames", "chan"), None),
        P(("frames", "chan")),
        P(("frames", "chan")),
        P(("frames", "chan")),
        P(("frames", "chan"), None),
        P(("frames", "chan")),
        P(("frames", "chan"), None),
        P(("frames", "chan")),
        P(("frames", "chan"), None),
        P(None, "chan", "frames"),
    )
    return jax.shard_map(
        on_device, mesh=mesh, in_specs=in_specs, out_specs=out_specs, check_vma=False
    )
```

profile of v0, /device:TPU:0, one launch (start us, length us, event | category | flops | bytes accessed | tf_op | source)
XLA Modules:
  0.0 1376.5 jit_solution(16712030767400900798)
XLA Ops:
  7.2 14.3 %convolution_convert_fusion.2 = bf16[1536,768]{1,0:T(8,128)(2,1)} fusion(bf16[3456,1536]{1,0:T(8,128)(2,1)} %bitcast.119, bf16[3456,768]{1,0:T(8,128)(2,1)} %bitcast.137), kind=kOutput, calls=%fused_computation.31 | convolution fusion | flops 8154906624 | bytes 18284544 | tf_op jit(solution)/shard_map/dot_general | solution.py:25
  23.2 49.2 %reduce-scatter.23.cloned.1.call-done = bf16[384,768]{1,0:T(8,128)(2,1)} async-done(((bf16[1536,768]{1,0:T(8,128)(2,1)}), bf16[384,768]{1,0:T(8,128)(2,1)}) %reduce-scatter.23.cloned.1.call-update) | async-done | bytes 589840 | tf_op jit(solution)/shard_map/reduce_scatter | solution.py:60
  72.5 1.6 fusion.36
  74.1 1.6 multiply_reduce_fusion.8
  76.3 1.8 convolution_convert_fusion.1
  80.8 5.9 bitcast_convert_fusion
  86.7 2.0 slice.18
  88.7 2.2 copy.58
  90.8 78.6 %all-gather.3.cloned.1.call-done = bf16[1536,1536]{1,0:T(8,128)(2,1)} async-done(((bf16[384,1536]{1,0:T(8,128)(2,1)}), bf16[1536,1536]{1,0:T(8,128)(2,1)}) %all-gather.3.cloned.1.call-update) | async-done | bytes 4718608 | tf_op jit(solution)/shard_map/all_gather | solution.py:76
  169.5 4.9 fusion.68
  174.4 4.3 copy.59
  178.7 4.3 copy.57
  183.0 15.1 %multiply_reduce_fusion.1 = (f32[12,384]{1,0:T(8,128)S(1)}, f32[12,384,1536]{2,1,0:T(8,128)}) fusion(bf16[384,12,64]{0,2,1:T(8,128)(2,1)} %bitcast.121, bf16[1536,12,64]{0,2,1:T(8,128)(2,1)} %bitcast.114), kind=kOutput, calls=%fused_computation.4 | convolution fusion | flops 920120832 | bytes 31279104 | tf_op jit(solution)/shard_map/qhd,khd->hqk/dot_general | solution.py:80
  198.1 12.9 exponential_reduce_fusion
  211.1 12.4 fusion.19
  225.5 2.1 convolution_add_fusion
  227.7 2.9 fusion.22
  231.8 17.6 %all_gather.10 = bf16[192,1536]{1,0:T(8,128)(2,1)} all-gather(bf16[192,384]{1,0:T(8,128)(2,1)S(1)} %fusion.30), channel_id=1, replica_groups=mesh['frames'=8,'chan'=4] {'chan'}, dimensions={1}, use_global_device_ids=true | all-gather | bytes 737280 | tf_op jit(solution)/shard_map/all_gather | solution.py:102
  249.4 1.9 reduce_max.19
  251.3 1.5 fusion.34
  253.0 19.7 %fusion.3 = (f32[3,64,1536]{2,1,0:T(8,128)S(1)}, bf16[18,64,1536]{2,1,0:T(8,128)(2,1)}, bf16[3,18,64]{2,1,0:T(8,128)(2,1)}, f32[3,18,64,1536]{3,2,1,0:T(8,128)}) fusion(bf16[1,3,18,64,1536]{4,3,2,1,0:T(8,128)(2,1)} %param.19, f32[18,64,1536]{2,1,0:T(8,128)} %bitcast_convert_fusion, f32[3,18,64]{2,1,0:T(8,128)S(1)} %copy-done.39, f32[3,64,1536]{2,1,0:T(8,128)S(1)} %fusion.33), kind=kLoop, calls=%fused_computation.9 | loop fusion | flops 40399488 | bytes 44847360 | tf_op jit(solution)/shard_map/reduce_sum | solution.py:114
  274.9 2.2 copy.66
  277.2 21.7 %reduce-scatter.35.cloned.1.call-done = bf16[384,192]{1,0:T(8,128)(2,1)} async-done(((bf16[1536,192]{1,0:T(8,128)(2,1)}), bf16[384,192]{1,0:T(8,128)(2,1)}) %reduce-scatter.35.cloned.1.call-update) | async-done | bytes 147472
  300.3 9.3 fusion.71
  309.6 6.1 multiply_reduce_fusion.2
  318.0 1.5 convolution_convert_fusion.4
  319.5 2.2 copy.60
  321.7 13.6 convolution_convert_fusion.3
  335.3 22.8 %multiply_reduce_fusion = (f32[12,384]{1,0:T(8,128)}, f32[12,384,1536]{2,1,0:T(8,128)}) fusion(f32[12,384,1536]{2,1,0:T(8,128)} %get-tuple-element.103, f32[12,384]{1,0:T(8,128)S(1)} %copy-done.22, bf16[384,12,64]{0,2,1:T(8,128)(2,1)S(1)} %bitcast.127, bf16[1536,12,64]{0,2,1:T(8,128)(2,1)S(1)} %bitcast.113), kind=kOutput, calls=%fused_computation.1 | convolution fusion | flops 934276608 | bytes 59609088 | tf_op jit(solution)/shard_map/qhd,khd->hqk/dot_general | solution.py:152
  358.0 23.5 %multiply_convert_fusion = bf16[12,384,1536]{2,1,0:T(8,128)(2,1)} fusion(f32[12,384,1536]{2,1,0:T(8,128)} %get-tuple-element.108, f32[12,384,1536]{2,1,0:T(8,128)} %get-tuple-element.103, f32[12,384]{1,0:T(8,128)} %get-tuple-element.107, f32[12,384]{1,0:T(8,128)} %copy-done.21), kind=kLoop, calls=%fused_computation | loop fusion | flops 35389440 | bytes 70815744 | tf_op jit(solution)/shard_map/convert_element_type | solution.py:156
  381.6 8.0 multiply_convert_fusion.1
  389.6 2.5 pad_maximum_fusion
  392.1 6.6 copy.68
  398.8 11.3 fusion.23
  410.1 73.3 %reduce-scatter.37.cloned.1.call-done = bf16[384,1536]{1,0:T(8,128)(2,1)} async-done(((bf16[1536,1536]{1,0:T(8,128)(2,1)}), bf16[384,1536]{1,0:T(8,128)(2,1)}) %reduce-scatter.37.cloned.1.call-update) | async-done | bytes 1179664
  483.4 2.4 copy.69
  485.8 4.4 multiply_reduce_fusion.3
  491.5 1.6 fusion.65
  493.3 2.1 copy.72
  495.4 48.9 %all-gather.5.cloned.1.call-done = bf16[1536,768]{1,0:T(8,128)(2,1)} async-done(((bf16[384,768]{1,0:T(8,128)(2,1)}), bf16[1536,768]{1,0:T(8,128)(2,1)}) %all-gather.5.cloned.1.call-update) | async-done | bytes 2359312 | tf_op jit(solution)/shard_map/all_gather | solution.py:185
  544.4 15.2 %fusion.6 = bf16[3456,768]{0,1:T(8,128)(2,1)} fusion(bf16[1536,768]{1,0:T(8,128)(2,1)} %all-gather.5.cloned.1.call-done, bf16[3456,1536]{1,0:T(8,128)(2,1)} %bitcast.120), kind=kOutput, calls=%fused_computation.17 | convolution fusion | flops 8156381184 | bytes 18284544 | tf_op jit(solution)/shard_map/dot_general | solution.py:25
  559.6 8.0 copy.63
  567.7 15.9 %copy.70 = bf16[3,18,64,768]{2,1,0,3:T(8,128)(2,1)} copy(bf16[3,18,64,768]{3,2,1,0:T(8,128)(2,1)} %bitcast.116) | data formatting | bytes 10616832
  583.5 15.7 %reshape.226 = bf16[768,3456]{1,0:T(8,128)(2,1)} reshape(bf16[768,3,18,64]{3,2,1,0:T(8,128)(2,1)} %bitcast.111) | data formatting | bytes 10616832
  599.3 2.4 fusion.48
  601.8 3.7 fusion.37
  606.6 9.9 fusion.40
  617.2 8.4 fusion.26
  626.3 7.1 fusion.31
  636.7 20.9 %copy.61 = f32[3456,1536]{0,1:T(8,128)} copy(f32[3456,1536]{1,0:T(8,128)} %bitcast.110) | data formatting | bytes 42467328 | tf_op jit(solution)/shard_map/mul | solution.py:112
  657.6 25.9 %all-reduce.8 = bf16[3,18,64]{1,2,0:T(8,128)(2,1)} all-reduce(bf16[3,18,64]{1,2,0:T(8,128)(2,1)} %copy.64), channel_id=20, replica_groups=mesh['frames'=8,'chan'=4] {'frames'}, use_global_device_ids=true, to_apply=%region_43.0.clone | all-reduce | flops 3456 | bytes 13824
  684.8 39.9 %all-reduce.9 = (f32[768]{0:T(1024)}, f32[768]{0:T(1024)}, f32[768]{0:T(1024)}, f32[768]{0:T(1024)}, f32[768]{0:T(1024)}, /*index=5*/f32[3072]{0:T(1024)}, f32[768]{0:T(1024)}) all-reduce(f32[768]{0:T(1024)} %get-tuple-element.75, f32[768]{0:T(1024)} %get-tuple-element.82, ...), channel_id=8, replica_groups=mesh['frames'=8,'chan'=4] {'frames','chan'}, use_global_device_ids=true, to_apply=%region_24.0.clone | all-reduce | flops 7680 | bytes 61440
  733.6 1.6 copy.73
  735.2 1.6 copy.65
  736.9 17.3 %fusion.4 = bf16[3456,1536]{0,1:T(8,128)(2,1)} fusion(f32[3456,1536]{0,1:T(8,128)} %copy.61, bf16[1536,768]{1,0:T(8,128)(2,1)} %all-gather.5.cloned.1.call-done, bf16[3456,768]{1,0:T(8,128)(2,1)} %bitcast.138), kind=kOutput, calls=%fused_computation.11 | convolution fusion | flops 8164343808 | bytes 39518208 | tf_op jit(solution)/shard_map/dot_general | solution.py:25
  754.2 14.4 %copy.62 = bf16[3456,1536]{1,0:T(8,128)(2,1)} copy(bf16[3456,1536]{0,1:T(8,128)(2,1)} %fusion.4) | data formatting | bytes 21233664 | tf_op jit(solution)/shard_map/convert_element_type | solution.py:192
  768.6 3.0 reshape.227
  771.6 3.6 copy.71
  775.2 2.6 convert_element_type.160
  777.8 84.2 %reduce-scatter.27.cloned.1.call-done = f32[24,768]{1,0:T(8,128)} async-done(((f32[768,768]{1,0:T(8,128)}), f32[24,768]{1,0:T(8,128)}) %reduce-scatter.27.cloned.1.call-update) | async-done | bytes 73744 | tf_op jit(solution)/shard_map/reduce_scatter | solution.py:223
  862.0 99.3 %reduce-scatter.43.cloned.1.call-done = f32[40,24]{0,1:T(8,128)} async-done(((f32[40,768]{0,1:T(8,128)}), f32[40,24]{0,1:T(8,128)}) %reduce-scatter.43.cloned.1.call-update) | async-done | bytes 3856
  961.3 142.3 %reduce-scatter.31.cloned.1.call-done = f32[96,768]{1,0:T(8,128)} async-done(((f32[3072,768]{1,0:T(8,128)}), f32[96,768]{1,0:T(8,128)}) %reduce-scatter.31.cloned.1.call-update) | async-done | bytes 294928 | tf_op jit(solution)/shard_map/reduce_scatter | solution.py:229
  1103.5 140.8 %reduce-scatter.29.cloned.1.call-done = f32[24,3072]{1,0:T(8,128)} async-done(((f32[768,3072]{1,0:T(8,128)}), f32[24,3072]{1,0:T(8,128)}) %reduce-scatter.29.cloned.1.call-update) | async-done | bytes 294928 | tf_op jit(solution)/shard_map/reduce_scatter | solution.py:227
  1244.3 125.5 %reduce-scatter.25.cloned.1.call-done = f32[24,2304]{1,0:T(8,128)} async-done(((f32[768,2304]{1,0:T(8,128)}), f32[24,2304]{1,0:T(8,128)}) %reduce-scatter.25.cloned.1.call-update) | async-done | bytes 221200 | tf_op jit(solution)/shard_map/reduce_scatter | solution.py:222
  (184 shorter events, 30.5 us)
Async XLA Ops:
  7.2 69.1 %copy-start = (bf16[768,2304]{1,0:T(8,128)(2,1)S(1)}, bf16[768,2304]{1,0:T(8,128)(2,1)}, u32[]{:S(2)}) copy-start(bf16[768,2304]{1,0:T(8,128)(2,1)} %param.26) | copy-start | bytes 10616836
  7.2 65.3 %reduce-scatter.23.cloned.1.call-start = ((), (), s32[]{:S(2)}) async-start(), calls=%async_computation.11 | async-start | bytes 2949120 | tf_op jit(solution)/shard_map/reduce_scatter | solution.py:60
  21.5 54.7 %copy-start.30 = (f32[768]{0:T(1024)S(1)}, f32[768]{0:T(1024)}, u32[]{:S(2)}) copy-start(f32[768]{0:T(1024)} %param.24) | copy-start | bytes 9220
  21.5 54.7 %copy-start.33 = (f32[768]{0:T(1024)S(1)}, f32[768]{0:T(1024)}, u32[]{:S(2)}) copy-start(f32[768]{0:T(1024)} %param.25) | copy-start | bytes 9220
  21.6 147.9 %all-gather.3.cloned.1.call-start = ((), (), s32[]{:S(2)}) async-start(), calls=%async_computation.12 | async-start | bytes 5898240 | tf_op jit(solution)/shard_map/all_gather | solution.py:76
  72.5 3.8 copy-start.9
  72.5 3.8 copy-start.12
  74.1 4.0 copy-start.35
  76.3 1.8 copy-start.40
  78.1 1.2 copy-start.23
  80.4 218.5 %reduce-scatter.35.cloned.1.call-start = ((), (), s32[]{:S(2)}) async-start(), calls=%async_computation.19 | async-start | bytes 983040
  198.1 12.9 copy-start.1
  198.1 27.3 %slice-start.2 = ((s8[4718592]{0:T(1024)(128)(4,1)}), s8[4194304]{0:T(1024)(128)(4,1)S(1)}, s32[]{:S(2)}) async-start(s8[4718592]{0:T(1024)(128)(4,1)} %bitcast.141), calls=%async_computation.26 | async-start | bytes 8388608
  211.0 12.5 copy-start.21
  211.0 12.5 copy-start.10
  211.0 12.5 copy-start.13
  211.0 12.5 copy-start.25
  211.1 12.5 copy-start.51
  211.1 14.4 %slice-start.3 = ((s8[4718592]{0:T(1024)(128)(4,1)}), s8[524288]{0:T(1024)(128)(4,1)S(1)}, s32[]{:S(2)}) async-start(s8[4718592]{0:T(1024)(128)(4,1)} %bitcast.141), calls=%async_computation.27 | async-start | bytes 1048576
  223.5 1.9 copy-start.27
  223.6 1.9 copy-start.28
  223.6 1.9 copy-start.50
  223.6 4.1 slice-start
  224.4 3.2 copy-start.5
  224.5 91.2 %copy-start.32 = (f32[384]{0:T(512)}, f32[384]{0:T(512)S(1)}, u32[]{:S(2)}) copy-start(f32[384]{0:T(512)S(1)} %broadcast_multiply_fusion.2) | copy-start | bytes 4612
  225.5 90.2 %copy-start.38 = (f32[384]{0:T(512)}, f32[384]{0:T(512)S(1)}, u32[]{:S(2)}) copy-start(f32[384]{0:T(512)S(1)} %fusion.54) | copy-start | bytes 4612
  225.5 2.2 slice-start.1
  225.5 2.2 copy-start.52
  227.7 2.9 copy-start.54
  227.7 3.7 copy-start.24
  251.3 1.5 copy-start.7
  251.3 1.8 copy-start.39
  272.7 1.1 copy-start.15
  277.2 206.3 %reduce-scatter.37.cloned.1.call-start = ((), (), s32[]{:S(2)}) async-start(), calls=%async_computation.20 | async-start | bytes 5898240
  300.3 15.9 %copy-start.17 = (f32[384,768]{1,0:T(8,128)}, f32[384,768]{1,0:T(8,128)S(1)}, u32[]{:S(2)}) copy-start(f32[384,768]{1,0:T(8,128)S(1)} %fusion.46) | copy-start | bytes 3538948
  300.3 9.3 copy-start.6
  309.6 6.1 copy-start.20
  309.6 6.1 copy-start.45
  316.2 1.9 copy-start.26
  317.0 1.0 copy-start.3
  321.7 13.6 copy-start.2
  321.7 13.6 copy-start.16
  321.7 13.6 copy-start.22
  381.6 8.0 copy-start.8
  398.7 145.6 %all-gather.5.cloned.1.call-start = ((), (), s32[]{:S(2)}) async-start(), calls=%async_computation.13 | async-start | bytes 2949120 | tf_op jit(solution)/shard_map/all_gather | solution.py:185
  410.1 75.7 %copy-start.31 = (f32[768]{0:T(1024)S(1)}, f32[768]{0:T(1024)}, u32[]{:S(2)}) copy-start(f32[768]{0:T(1024)} %param.24) | copy-start | bytes 9220
  410.1 75.7 %copy-start.36 = (f32[384]{0:T(512)S(1)}, f32[384]{0:T(512)}, u32[]{:S(2)}) copy-start(f32[384]{0:T(512)} %copy-done.35) | copy-start | bytes 4612
  485.8 4.5 copy-start.43
  485.8 4.5 copy-start.11
  485.8 4.5 copy-start.14
  485.8 4.5 copy-start.41
  490.3 1.3 copy-start.4
  493.2 240.4 %reduce-scatter.41.cloned.1.call-start = ((), (), s32[]{:S(2)}) async-start(), calls=%async_computation.22 | async-start | bytes 663552
  495.4 273.3 %reduce-scatter.39.cloned.1.call-start = ((), (), s32[]{:S(2)}) async-start(), calls=%async_computation.21 | async-start | bytes 5971968
  599.3 178.5 %reduce-scatter.33.cloned.1.call-start = ((), (), s32[]{:S(2)}) async-start(), calls=%async_computation.18 | async-start | bytes 811008 | tf_op jit(solution)/shard_map/reduce_scatter | solution.py:231
  601.8 260.3 %reduce-scatter.27.cloned.1.call-start = ((), (), s32[]{:S(2)}) async-start(), calls=%async_computation.15 | async-start | bytes 2433024 | tf_op jit(solution)/shard_map/reduce_scatter | solution.py:223
  605.5 355.8 %reduce-scatter.43.cloned.1.call-start = ((), (), s32[]{:S(2)}) async-start(), calls=%async_computation.23 | async-start | bytes 405504
  606.5 497.0 %reduce-scatter.31.cloned.1.call-start = ((), (), s32[]{:S(2)}) async-start(), calls=%async_computation.17 | async-start | bytes 9732096 | tf_op jit(solution)/shard_map/reduce_scatter | solution.py:229
  616.5 627.8 %reduce-scatter.29.cloned.1.call-start = ((), (), s32[]{:S(2)}) async-start(), calls=%async_computation.16 | async-start | bytes 9732096 | tf_op jit(solution)/shard_map/reduce_scatter | solution.py:227
  625.6 744.1 %reduce-scatter.25.cloned.1.call-start = ((), (), s32[]{:S(2)}) async-start(), calls=%async_computation.14 | async-start | bytes 7299072 | tf_op jit(solution)/shard_map/reduce_scatter | solution.py:222
  636.7 48.1 %copy-start.46 = (f32[768]{0:T(1024)S(1)}, f32[768]{0:T(1024)}, u32[]{:S(2)}) copy-start(f32[768]{0:T(1024)} %get-tuple-element.80) | copy-start | bytes 9220
  636.7 48.1 %copy-start.47 = (f32[768]{0:T(1024)S(1)}, f32[768]{0:T(1024)}, u32[]{:S(2)}) copy-start(f32[768]{0:T(1024)} %get-tuple-element.100) | copy-start | bytes 9220
  636.7 48.1 %copy-start.48 = (f32[768]{0:T(1024)S(1)}, f32[768]{0:T(1024)}, u32[]{:S(2)}) copy-start(f32[768]{0:T(1024)} %get-tuple-element.77) | copy-start | bytes 9220
  636.7 48.1 %copy-start.49 = (f32[768]{0:T(1024)S(1)}, f32[768]{0:T(1024)}, u32[]{:S(2)}) copy-start(f32[768]{0:T(1024)} %get-tuple-element.79) | copy-start | bytes 9220
  (8 other events, 5.7 us)
Sparse Core Ops, SparseCore 0:
  21.7 50.7 reduce-scatter.22
  80.6 88.8 all-gather.2
  277.3 21.5 reduce-scatter.34
  398.9 84.5 reduce-scatter.36
  493.3 51.0 all-gather.4
  547.3 33.1 reduce-scatter.40
  599.4 55.7 reduce-scatter.38
  661.7 95.4 reduce-scatter.32
  763.9 98.1 reduce-scatter.26
  867.4 93.8 reduce-scatter.42
  968.8 134.7 reduce-scatter.30
  1109.9 134.3 reduce-scatter.28
  1251.5 118.2 reduce-scatter.24
where the time goes:
time: 1390 us; the launch traced here: 1380 us
  waiting for transfers between devices  864 us (62%)
  matrix products  193 us (14%)
  local copies, waits for them, and re-layouts  137 us (10%)
  blocking collectives  83.4 us (6%)
  other arithmetic  81.6 us (6%)
  between operations  16.1 us (1%)
    unnamed x18, waiting for transfers between devices  194 us
    reduce_scatter x1, waiting for transfers between devices, on_device(): lax.psum_scatter(down_grad, ('frames', 'chan'), scatter_dimension=0, tile...  142 us
    reduce_scatter x1, waiting for transfers between devices, on_device(): lax.psum_scatter(up_grad, ('frames', 'chan'), scatter_dimension=0, tiled=...  141 us
    reduce_scatter x1, waiting for transfers between devices, on_device(): lax.psum_scatter(attend_grad, ('frames', 'chan'), scatter_dimension=0, ti...  125 us
    dot_general x15, matrix products, tensor_dot_routine(): lax.dot_general(left, right, (((left_dim,), (right_dim,)), ((), ())), pre...  102 us
    reduce_scatter x1, waiting for transfers between devices, on_device(): lax.psum_scatter(out_grad, ('frames', 'chan'), scatter_dimension=0, tiled...  84.2 us
    all_gather x1, waiting for transfers between devices, on_device(): lax.all_gather(packed[:, model_width:], 'chan', axis=0, tiled=True)  78.6 us
    unnamed x136, local copies, waits for them, and re-layouts  71.7 us
  transfers between devices with their start and end apart: 13, of which 10 were waited for; matrix products, arithmetic and copies ran while one was open for 14% of the time, Pallas kernels for 0%

commit v1 on v0

v1 whole, which is shorter than its diff:
```python
from functools import partial

import jax
import jax.numpy as jnp
from jax import lax
from jax.experimental import pallas as pl
from jax.experimental.pallas import tpu as pltpu
from jax.sharding import PartitionSpec as P

HEADS = 12
HEAD_DIM = 64
EXP = 3
PIX = 64
LOG2E = 1.4426950408889634

epsilon = 1e-05
BF = jnp.bfloat16
F32 = jnp.float32


def dot(left, right, left_dim, right_dim):
    return lax.dot_general(
        left, right, (((left_dim,), (right_dim,)), ((), ())), preferred_element_type=F32
    )


class Plan:
    def __init__(self, frames, chan):
        self.frames, self.chan, self.half = frames, chan, chan // 2

    def pairs(self, target):
        return [
            (f * self.chan + z, (lambda t: t[0] * self.chan + t[1])(target(f, z)))
            for f in range(self.frames)
            for z in range(self.chan)
        ]

    def swap_frame(self, x, bit):
        return lax.ppermute(x, ("frames", "chan"), self.pairs(lambda f, z: (f ^ bit, z)))

    def swap_chan(self, x, bit):
        return lax.ppermute(x, ("frames", "chan"), self.pairs(lambda f, z: (f, z ^ bit)))

    def worker(self, f, r):
        return (f & ~1) + r % 2, (f & 1) * self.half + r // 2

    def to_worker(self, x, s):
        return lax.ppermute(
            x, ("frames", "chan"), self.pairs(lambda f, z: self.worker(f, z ^ s))
        )

    def from_worker(self, x, s):
        pairs = self.pairs(lambda f, z: self.worker(f, z ^ s))
        return lax.ppermute(x, ("frames", "chan"), [(d, o) for o, d in pairs])


def bits_of(n):
    return [1 << i for i in range(n.bit_length() - 1)]


def attend_kernel(q_ref, k_ref, v_ref, o_ref, e_ref, rinv_ref):
    scale = HEAD_DIM ** (-0.5) * LOG2E
    for h in range(q_ref.shape[1] // HEAD_DIM):
        cols = slice(h * HEAD_DIM, (h + 1) * HEAD_DIM)
        s = dot(q_ref[:, cols], k_ref[:, cols], 1, 1)
        m = jnp.max(s, axis=1, keepdims=True)
        e = jnp.exp2((s - m) * scale)
        total = jnp.sum(e, axis=1, keepdims=True)
        low = e.astype(BF)
        e_ref[h] = low
        o = dot(low, v_ref[:, cols], 1, 0)
        rinv = jnp.broadcast_to(1.0 / total, o.shape)
        rinv_ref[:, cols] = rinv
        o_ref[:, cols] = (o * rinv).astype(BF)


def attend(q, kv):
    rows, width = q.shape
    keys = kv.shape[0]
    lanes = 2 * HEAD_DIM
    steps = width // lanes
    return pl.pallas_call(
        attend_kernel,
        grid=(steps,),
        in_specs=[
            pl.BlockSpec((rows, lanes), lambda i: (0, i)),
            pl.BlockSpec((keys, lanes), lambda i: (0, i)),
            pl.BlockSpec((keys, lanes), lambda i: (0, i + steps)),
        ],
        out_specs=[
            pl.BlockSpec((rows, lanes), lambda i: (0, i)),
            pl.BlockSpec((2, rows, keys), lambda i: (i, 0, 0)),
            pl.BlockSpec((rows, lanes), lambda i: (0, i)),
        ],
        out_shape=[
            jax.ShapeDtypeStruct((rows, width), BF),
            jax.ShapeDtypeStruct((HEADS, rows, keys), BF),
            jax.ShapeDtypeStruct((rows, width), F32),
        ],
        compiler_params=pltpu.CompilerParams(vmem_limit_bytes=48 << 20),
        cost_estimate=pl.CostEstimate(
            flops=16 * rows * keys * width, bytes_accessed=24 << 20, transcendentals=0
        ),
        name="attend",
    )(q, kv, kv)


def attend_back_kernel(q_ref, k_ref, v_ref, o_ref, do_ref, e_ref, rinv_ref, dq_ref, dk_ref, dv_ref):
    scale = HEAD_DIM ** (-0.5)
    for h in range(q_ref.shape[1] // HEAD_DIM):
        cols = slice(h * HEAD_DIM, (h + 1) * HEAD_DIM)
        do = do_ref[:, cols].astype(F32) * rinv_ref[:, cols]
        inner = jnp.sum(do * o_ref[:, cols].astype(F32), axis=1, keepdims=True)
        do = do.astype(BF)
        e = e_ref[h]
        dp = dot(do, v_ref[:, cols], 1, 1)
        ds = (e.astype(F32) * (dp - inner)).astype(BF)
        dq_ref[:, cols] = (dot(ds, k_ref[:, cols], 1, 0) * scale).astype(BF)
        dk_ref[:, cols] = (dot(ds, q_ref[:, cols], 0, 0) * scale).astype(BF)
        dv_ref[:, cols] = dot(e, do, 0, 0).astype(BF)


def attend_back(q, kv, o, do, e, rinv):
    rows, width = q.shape
    keys = kv.shape[0]
    lanes = 2 * HEAD_DIM
    steps = width // lanes
    row_spec = pl.BlockSpec((rows, lanes), lambda i: (0, i))
    key_spec = pl.BlockSpec((keys, lanes), lambda i: (0, i))
    return pl.pallas_call(
        attend_back_kernel,
        grid=(steps,),
        in_specs=[
            row_spec,
            key_spec,
            pl.BlockSpec((keys, lanes), lambda i: (0, i + steps)),
            row_spec,
            row_spec,
            pl.BlockSpec((2, rows, keys), lambda i: (i, 0, 0)),
            row_spec,
        ],
        out_specs=[row_spec, key_spec, key_spec],
        out_shape=[
            jax.ShapeDtypeStruct((rows, width), BF),
            jax.ShapeDtypeStruct((keys, width), BF),
            jax.ShapeDtypeStruct((keys, width), BF),
        ],
        compiler_params=pltpu.CompilerParams(vmem_limit_bytes=48 << 20),
        cost_estimate=pl.CostEstimate(
            flops=40 * rows * keys * width, bytes_accessed=32 << 20, transcendentals=0
        ),
        name="attend_back",
    )(q, kv, kv, o, do, e, rinv)


def blend_kernel(
    chunk_ref, logit_ref, fields_ref, cot_ref, offset_ref, *rest
):
    mixed_ref, gate_ref, part_ref, bias_ref, total = rest[-5:]
    step = pl.program_id(0)
    channels = cot_ref.shape[0]

    @pl.when(step == 0)
    def _():
        a, b, c = (logit_ref[e * PIX : (e + 1) * PIX, :].astype(F32) for e in range(EXP))
        m = jnp.maximum(jnp.maximum(a, b), c)
        a, b, c = jnp.exp(a - m), jnp.exp(b - m), jnp.exp(c - m)
        scale = 1.0 / (a + b + c)
        for e, x in enumerate((a, b, c)):
            gate_ref[e * PIX : (e + 1) * PIX, :] = x * scale
        total[...] = jnp.zeros_like(total)

    high = 16
    for i in range(0, PIX, high):
        gates = [gate_ref[e * PIX + i : e * PIX + i + high, :] for e in range(EXP)]
        sums = [total[e * PIX + i : e * PIX + i + high, :] for e in range(EXP)]
        for c in range(channels):
            g = cot_ref[c, i : i + high, :].astype(F32)
            mixed = None
            for e in range(EXP):
                x = fields_ref[e, c, i : i + high, :].astype(F32) + offset_ref[e, c, i : i + high, :]
                term = gates[e] * x
                mixed = term if mixed is None else mixed + term
                sums[e] = sums[e] + g * x
                bias_ref[e, c, i : i + high, :] = jnp.sum(gates[e] * g, axis=1, keepdims=True)
            mixed_ref[c, i : i + high, :] = mixed.astype(BF)
        for e in range(EXP):
            total[e * PIX + i : e * PIX + i + high, :] = sums[e]

    @pl.when(step == pl.num_programs(0) - 1)
    def _():
        gates = [gate_ref[e * PIX : (e + 1) * PIX, :] for e in range(EXP)]
        sums = [total[e * PIX : (e + 1) * PIX, :] for e in range(EXP)]
        inner = gates[0] * sums[0] + gates[1] * sums[1] + gates[2] * sums[2]
        for e in range(EXP):
            part_ref[e * PIX : (e + 1) * PIX, :] = (gates[e] * (sums[e] - inner)).astype(BF)


def blend(chunk, logits, fields, cot, offset, mixed):
    channels, pixels, patches = cot.shape
    rows = logits.shape[1]
    block = max(b for b in (6, 3, 2, 1) if channels % b == 0)
    wide = pl.BlockSpec((EXP * PIX, rows), lambda i, r: (0, 0))
    in_specs = [
        wide,
        pl.BlockSpec((EXP, block, PIX, rows), lambda i, r: (0, i, 0, r[0])),
        pl.BlockSpec((block, PIX, rows), lambda i, r: (i, 0, r[0])),
        pl.BlockSpec((EXP, block, PIX, 1), lambda i, r: (0, i, 0, 0)),
    ]
    operands = [chunk, logits, fields, cot, offset]
    aliases = {}
    if mixed is not None:
        in_specs.append(pl.BlockSpec(memory_space=pl.ANY))
        operands.append(mixed)
        aliases = {5: 0}
    return pl.pallas_call(
        blend_kernel,
        grid_spec=pltpu.PrefetchScalarGridSpec(
            num_scalar_prefetch=1,
            grid=(channels // block,),
            in_specs=in_specs,
            out_specs=[
                pl.BlockSpec((block, PIX, rows), lambda i, r: (i, 0, r[0])),
                wide,
                wide,
                pl.BlockSpec((EXP, block, PIX, 1), lambda i, r: (0, i, 0, 0)),
            ],
            scratch_shapes=[pltpu.VMEM((EXP * PIX, rows), F32)],
        ),
        out_shape=[
            jax.ShapeDtypeStruct(cot.shape, BF),
            jax.ShapeDtypeStruct((EXP * PIX, rows), F32),
            jax.ShapeDtypeStruct((EXP * PIX, rows), BF),
            jax.ShapeDtypeStruct((EXP, channels, PIX, 1), F32),
        ],
        input_output_aliases=aliases,
        compiler_params=pltpu.CompilerParams(vmem_limit_bytes=40 << 20),
        cost_estimate=pl.CostEstimate(flops=8 << 20, bytes_accessed=6 << 20, transcendentals=0),
        name="blend",
    )(*operands)


def fields_back_kernel(chunk_ref, weight_ref, start_ref, gate_ref, cot_ref, *rest):
    out_ref = rest[-1]
    grad = dot(weight_ref[0], start_ref[...], 1, 1)
    gate = gate_ref[...]
    for c in range(cot_ref.shape[0]):
        lines = slice(c * PIX, (c + 1) * PIX)
        out_ref[0, lines, :] = (grad[lines, :] + gate * cot_ref[c].astype(F32)).astype(BF)


def fields_back(chunk, weight, start, gates, cot, grad):
    channels, pixels, patches = cot.shape
    rows = gates.shape[1]
    width = weight.shape[2]
    block = max(b for b in (6, 3, 2, 1) if channels % b == 0)
    in_specs = [
        pl.BlockSpec((1, block * PIX, width), lambda e, i, r: (e, i, 0)),
        pl.BlockSpec((rows, width), lambda e, i, r: (0, 0)),
        pl.BlockSpec((PIX, rows), lambda e, i, r: (e, 0)),
        pl.BlockSpec((block, PIX, rows), lambda e, i, r: (i, 0, r[0])),
    ]
    operands = [chunk, weight, start, gates, cot]
    aliases = {}
    if grad is not None:
        in_specs.append(pl.BlockSpec(memory_space=pl.ANY))
        operands.append(grad)
        aliases = {5: 0}
    return pl.pallas_call(
        fields_back_kernel,
        grid_spec=pltpu.PrefetchScalarGridSpec(
            num_scalar_prefetch=1,
            grid=(EXP, channels // block),
            in_specs=in_specs,
            out_specs=pl.BlockSpec((1, block * PIX, rows), lambda e, i, r: (e, i, r[0])),
        ),
        out_shape=jax.ShapeDtypeStruct((EXP, channels * PIX, patches), BF),
        input_output_aliases=aliases,
        compiler_params=pltpu.CompilerParams(vmem_limit_bytes=40 << 20),
        cost_estimate=pl.CostEstimate(
            flops=2 * EXP * channels * PIX * rows * width, bytes_accessed=10 << 20, transcendentals=0
        ),
        name="fields_back",
    )(*operands)


def norm_parts(v):
    centred = v - jnp.mean(v, axis=-1, keepdims=True)
    spread = jnp.mean(centred * centred, axis=-1, keepdims=True)
    r = lax.rsqrt(spread + epsilon)
    return centred * r, r


def norm_back(grad, n, r, gain):
    t = grad * gain
    return r * (
        t - jnp.mean(t, axis=-1, keepdims=True) - n * jnp.mean(t * n, axis=-1, keepdims=True)
    )


def add_low(a, b):
    return (a.astype(F32) + b.astype(F32)).astype(BF)


def halve(x, axis, mine):
    keep = lax.dynamic_index_in_dim(x, mine, axis, keepdims=False)
    send = lax.dynamic_index_in_dim(x, 1 - mine, axis, keepdims=False)
    return keep, send


def frame_levels(plan, x, bits, f):
    left = sorted(bits, reverse=True)
    for bit in bits:
        axis = left.index(bit)
        keep, send = halve(x, axis, (f // bit) % 2)
        x = add_low(keep, plan.swap_frame(send, bit))
        left.remove(bit)
    return x


def chan_levels(plan, x, z):
    bits = bits_of(plan.chan)
    x = x.reshape((2,) * len(bits) + x.shape[1:])
    left = sorted(bits, reverse=True)
    for bit in bits:
        axis = left.index(bit)
        keep, send = halve(x, axis, (z // bit) % 2)
        x = add_low(keep, plan.swap_chan(send, bit))
        left.remove(bit)
    return x


def core_product(plan, left, right, f):
    rows, columns = left.shape
    parts = left.reshape(rows, plan.frames // 2, 2, columns // plan.frames)
    keep, send = halve(parts, 2, f % 2)
    keep, send = (a.reshape(rows, columns // 2) for a in (keep, send))
    far = plan.swap_frame(dot(send, right, 0, 0).astype(BF), 1)
    both = (dot(keep, right, 0, 0) + far.astype(F32)).astype(BF)
    return both.reshape(plan.frames // 2, columns // plan.frames, right.shape[1])


def high_axes(plan, x):
    return x.reshape((2,) * (len(bits_of(plan.frames)) - 1) + x.shape[1:])


def on_device(
    plan,
    fields,
    lead_index,
    embed_weight,
    position_embed,
    lead_table,
    attend_gain,
    attend_shift,
    attend_weight,
    out_weight,
    out_bias,
    mixer_gain,
    mixer_shift,
    up_weight,
    up_bias,
    down_weight,
    down_bias,
    head_weight,
    specialist_cell_offset,
    cotangent,
):
    f, z = lax.axis_index("frames"), lax.axis_index("chan")
    chan, frames = plan.chan, plan.frames
    width = attend_gain.shape[0]
    channels, pixels, patches = cotangent.shape[1:]
    rows = position_embed.shape[0]
    lines = EXP * channels * PIX
    own_fields, cot = fields[0], cotangent[0]
    flat_fields = own_fields.reshape(lines, patches)
    flat_weight = embed_weight.reshape(lines, width)

    onehot = (
        lead_index[:, None] == jnp.arange(lead_table.shape[0], dtype=jnp.int32)[None, :]
    ).astype(BF)
    lead_vector = dot(onehot, lead_table, 1, 0)
    got = []
    for s in range(chan):
        block = lax.dynamic_slice(flat_fields, (0, (z ^ s) * rows), (lines, rows))
        part = dot(block, flat_weight, 0, 0)
        if s == 0:
            part = part + position_embed.astype(F32) + lead_vector
        got.append(plan.to_worker(part.astype(BF), s))
    stream_start = sum(a.astype(F32) for a in got)

    first_n, first_r = norm_parts(stream_start)
    normed_first = (first_n * attend_gain + attend_shift).astype(BF)
    chunks = [normed_first]
    for bit in bits_of(plan.half):
        chunks += [plan.swap_chan(a, bit) for a in chunks]
    every = []
    for a in chunks:
        every += [a, plan.swap_frame(a, 1)]
    normed_every = jnp.concatenate(every, axis=0)
    queries = dot(normed_first, attend_weight[:, :width], 1, 0).astype(BF)
    keys_values = dot(normed_every, attend_weight[:, width:], 1, 0).astype(BF)
    attended, shares, rinv = attend(queries, keys_values)

    stream_mid = stream_start + dot(attended, out_weight, 1, 0) + out_bias
    second_n, second_r = norm_parts(stream_mid)
    normed_second = (second_n * mixer_gain + mixer_shift).astype(BF)
    hidden = dot(normed_second, up_weight, 1, 0) + up_bias
    active = jax.nn.gelu(hidden, approximate=True).astype(BF)
    end_low = (stream_mid + dot(active, down_weight, 1, 0) + down_bias).astype(BF)
    logits = dot(head_weight, end_low, 0, 1).astype(BF)

    offset = specialist_cell_offset[..., None]
    numbers = [(z ^ s).astype(jnp.int32)[None] for s in range(chan)]
    near = [plan.from_worker(logits, s) for s in range(chan)]
    mixed, gates, bias_parts, back = None, [], [], []
    for s in range(chan):
        mixed, gate, part, bias = blend(numbers[s], near[s], own_fields, cot, offset, mixed)
        gates.append(gate)
        bias_parts.append(bias)
        back.append(plan.to_worker(part, s))
    expert_bias = sum(bias_parts)[..., 0]
    logit_low = sum(a.astype(F32) for a in back).astype(BF)

    end_grad = dot(logit_low, head_weight, 0, 1)
    down_bias_grad = jnp.sum(end_grad, axis=0)
    down_low = end_grad.astype(BF)
    active_grad = dot(down_low, down_weight, 1, 1)
    gelu_pull = jax.vjp(partial(jax.nn.gelu, approximate=True), hidden)[1]
    hidden_grad = gelu_pull(active_grad)[0]
    up_bias_grad = jnp.sum(hidden_grad, axis=0)
    hidden_low = hidden_grad.astype(BF)
    second_grad = dot(hidden_low, up_weight, 1, 1)
    mixer_gain_grad = jnp.sum(second_grad * second_n, axis=0)
    mixer_shift_grad = jnp.sum(second_grad, axis=0)
    mid_grad = end_grad + norm_back(second_grad, second_n, second_r, mixer_gain)
    out_bias_grad = jnp.sum(mid_grad, axis=0)
    branch_low = mid_grad.astype(BF)
    attended_low = dot(branch_low, out_weight, 1, 1).astype(BF)

    query_low, key_low, value_low = attend_back(
        queries, keys_values, attended, attended_low, shares, rinv
    )
    key_value_low = jnp.concatenate([key_low, value_low], axis=1)
    far_grad = dot(key_value_low, attend_weight[:, width:], 1, 1)
    parts = [far_grad[i * rows : (i + 1) * rows] for i in range(chan)]
    parts[0] = parts[0] + dot(query_low, attend_weight[:, :width], 1, 1)
    parts = [
        parts[2 * i] + plan.swap_frame(parts[2 * i + 1].astype(BF), 1).astype(F32)
        for i in range(plan.half)
    ]
    for bit in reversed(bits_of(plan.half)):
        parts = [
            parts[i] + plan.swap_chan(parts[i + bit].astype(BF), bit).astype(F32)
            for i in range(bit)
        ]
    first_grad = parts[0]
    attend_gain_grad = jnp.sum(first_grad * first_n, axis=0)
    attend_shift_grad = jnp.sum(first_grad, axis=0)
    start_grad = mid_grad + norm_back(first_grad, first_n, first_r, attend_gain)

    vectors = jnp.stack(
        [
            attend_gain_grad,
            attend_shift_grad,
            mixer_gain_grad,
            mixer_shift_grad,
            out_bias_grad,
            down_bias_grad,
        ]
    )
    n_up = up_bias.shape[0] // width
    vectors = jnp.concatenate([vectors, up_bias_grad.reshape(width, n_up).T], axis=0)
    n_vectors = vectors.shape[0]
    vectors = jnp.pad(vectors, ((0, 16 - n_vectors), (0, 0)))
    sent = jnp.concatenate([start_grad, vectors], axis=0).astype(BF)
    got = [plan.from_worker(sent, s) for s in range(chan)]
    fields_grad = None
    for s in range(chan):
        fields_grad = fields_back(
            numbers[s], embed_weight.reshape(EXP, channels * PIX, width), got[s], gates[s], cot, fields_grad
        )
    ordered = []
    for r in range(chan):
        choice = got[0]
        for s in range(1, chan):
            choice = jnp.where(z == r ^ s, got[s], choice)
        ordered.append(choice[:rows])
    start_every = jnp.concatenate(ordered, axis=0)
    vector_sum = sum(a[rows:].astype(F32) for a in got)
    lead_sum = jnp.sum(start_every.astype(F32), axis=0)

    per = width // frames
    small = jnp.concatenate(
        [vector_sum, onehot[0].astype(F32)[:, None] * lead_sum[None, :]], axis=0
    )
    n_small = small.shape[0]
    n_bias = EXP * channels
    bias_here = expert_bias.reshape(n_bias, frames, PIX // frames)
    bias_here = jnp.pad(
        jnp.transpose(bias_here, (1, 2, 0)), ((0, 0), (0, per - PIX // frames), (0, 0))
    )
    extra = jnp.concatenate(
        [got[0][:rows].T, small.T.astype(BF), bias_here.reshape(width, n_bias).astype(BF)], axis=1
    )
    extra = jnp.pad(extra, ((0, 0), (0, -extra.shape[1] % 128)))
    n_extra = extra.shape[1]
    embed_sum = core_product(plan, start_every, flat_fields.T, f)
    keep, send = halve(extra.reshape(frames // 2, 2, per, n_extra), 1, f % 2)
    extra = add_low(keep, plan.swap_frame(send, 1))
    high = bits_of(frames)[1:]
    cut = (lines + n_extra) // 256 * 128
    parts = [embed_sum[:, :, :cut], jnp.concatenate([embed_sum[:, :, cut:], extra], axis=2)]
    parts = [
        frame_levels(plan, high_axes(plan, a), order, f)
        for a, order in zip(parts, (high, high[::-1]))
    ]
    tail = jnp.concatenate(parts, axis=1).astype(F32)
    embed_out = tail[:, :lines].T.reshape(EXP, channels, PIX, per)
    position_out = tail[:, lines : lines + rows].T
    small_out = lax.dynamic_slice_in_dim(
        tail[:, lines + rows : lines + rows + n_small], z * (per // chan), per // chan, 0
    )
    vectors_out = [small_out[:, i] for i in range(6)]
    up_bias_out = small_out[:, 6 : 6 + n_up].reshape(-1)
    table_out = small_out[:, 16:].T
    bias_out = tail[: PIX // frames, lines + rows + n_small : lines + rows + n_small + n_bias]
    bias_out = bias_out.T.reshape(EXP, channels, PIX // frames)

    down_sum = core_product(plan, active, down_low, f)
    wide_sum = [
        core_product(plan, normed_second, hidden_low, f),
        core_product(plan, attended, branch_low, f),
        core_product(plan, end_low, logit_low.T, f),
    ]
    wide_sum = jnp.concatenate(wide_sum, axis=2)
    attend_sum = jnp.concatenate(
        [
            core_product(plan, normed_first, query_low, f),
            core_product(plan, normed_every, key_value_low, f),
        ],
        axis=2,
    )
    down_sum = frame_levels(plan, high_axes(plan, down_sum), high, f)
    wide_sum = frame_levels(plan, high_axes(plan, wide_sum), high[::-1], f)
    cut = attend_sum.shape[2] // 2
    attend_sum = jnp.concatenate(
        [
            frame_levels(plan, high_axes(plan, attend_sum[:, :, :cut]), high, f),
            frame_levels(plan, high_axes(plan, attend_sum[:, :, cut:]), high[::-1], f),
        ],
        axis=1,
    )
    down_sum = chan_levels(plan, down_sum.reshape(chan, -1, width), z).astype(F32)
    wide_sum = chan_levels(plan, wide_sum.reshape(chan, -1, wide_sum.shape[1]), z).astype(F32)
    attend_sum = chan_levels(plan, attend_sum.reshape(chan, -1, 3 * width), z).astype(F32)
    n_ff = up_bias.shape[0]

    return (
        mixed[None],
        fields_grad.reshape(fields.shape),
        embed_out,
        position_out,
        table_out,
        vectors_out[0],
        vectors_out[1],
        attend_sum,
        wide_sum[:, n_ff : n_ff + width],
        vectors_out[4],
        vectors_out[2],
        vectors_out[3],
        wide_sum[:, :n_ff],
        up_bias_out,
        down_sum,
        vectors_out[5],
        wide_sum[:, n_ff + width :],
        bias_out,
    )


def solution(mesh):
    plan = Plan(mesh.shape["frames"], mesh.shape["chan"])
    both = ("frames", "chan")
    in_specs = (
        P("frames", None, "chan", None, None),
        P("frames"),
        P(None, "chan", None, None),
        P("chan", None),
        *[P()] * 13,
        P(None, "chan", None),
        P("frames", "chan", None, None),
    )
    out_specs = (
        P("frames", "chan", None, None),
        P("frames", None, "chan", None, None),
        P(None, "chan", None, "frames"),
        P("chan", "frames"),
        P(None, both),
        P(both),
        P(both),
        P(both, None),
        P(both, None),
        P(both),
        P(both),
        P(both),
        P(both, None),
        P(both),
        P(both, None),
        P(both),
        P(both, None),
        P(None, "chan", "frames"),
    )
    return jax.shard_map(
        partial(on_device, plan), mesh=mesh, in_specs=in_specs, out_specs=out_specs, check_vma=False
    )
```

time: 1390 us -> 573 us (0.41)
  waiting for transfers between devices: 864 us -> 116 us
  Pallas kernels: 0 us -> 91.8 us
  starting transfers between devices: 1.01 us -> 92.7 us
  blocking collectives: 83.4 us -> 0 us
  matrix products: 193 us -> 122 us
  other arithmetic: 81.6 us -> 35.3 us
  local copies, waits for them, and re-layouts: 137 us -> 108 us
    reduce_scatter x6 -> x0, waiting for transfers between devices: 542 us -> none  [the longest x1 142 us: on_device(): lax.psum_scatter(down_grad, ('frames', 'chan'), scatter_dimension=0, tile...]
    unnamed x18 -> x0, waiting for transfers between devices: 194 us -> none
    all_gather x2 -> x0, waiting for transfers between devices: 128 us -> none  [the longest x1 78.6 us: on_device(): lax.all_gather(packed[:, model_width:], 'chan', axis=0, tiled=True)]
    ppermute x0 -> x48, waiting for transfers between devices: none -> 116 us  [the longest x24 55.9 us: swap_frame(): lax.ppermute(x, ('frames', 'chan'), self.pairs(lambda f, z: (f ^ bit, z)))]
    ppermute x0 -> x48, starting transfers between devices: none -> 92.7 us  [the longest x8 30.8 us: swap_chan(): lax.ppermute(x, ('frames', 'chan'), self.pairs(lambda f, z: (f, z ^ bit)))]
    pallas_call x0 -> x10, Pallas kernels: none -> 91.8 us  [the longest x4 28.6 us: blend(): pl.pallas_call(blend_kernel, grid_spec=pltpu.PrefetchScalarGridSpec(num_s...]
    dot_general x25 -> x31, matrix products: 193 us -> 122 us  [dot(): lax.dot_general(left, right, (((left_dim,), (right_dim,)), ((), ())), pre...]
    unnamed x2 -> x0, blocking collectives: 65.8 us -> none
  transfers between devices with their start and end apart: 13 -> 48, of which waited for: 10 -> 18; matrix products, arithmetic and copies ran while one was open for 14% -> 33% of each run, Pallas kernels for 0% -> 7%
where the time goes in v1:
time: 573 us; the launch traced here: 569 us
  matrix products  122 us (21%)
  waiting for transfers between devices  116 us (20%)
  local copies, waits for them, and re-layouts  108 us (19%)
  starting transfers between devices  92.7 us (16%)
  Pallas kernels  91.8 us (16%)
  other arithmetic  35.3 us (6%)
    dot_general x31, matrix products, dot(): lax.dot_general(left, right, (((left_dim,), (right_dim,)), ((), ())), pre...  122 us
    ppermute x24, waiting for transfers between devices, swap_frame(): lax.ppermute(x, ('frames', 'chan'), self.pairs(lambda f, z: (f ^ bit, z)))  55.9 us
    unnamed x222, local copies, waits for them, and re-layouts  34.6 us
    ppermute x8, starting transfers between devices, swap_chan(): lax.ppermute(x, ('frames', 'chan'), self.pairs(lambda f, z: (f, z ^ bit)))  30.8 us
    ppermute x24, starting transfers between devices, swap_frame(): lax.ppermute(x, ('frames', 'chan'), self.pairs(lambda f, z: (f ^ bit, z)))  29.5 us
    pallas_call x4, Pallas kernels, blend(): pl.pallas_call(blend_kernel, grid_spec=pltpu.PrefetchScalarGridSpec(num_s...  28.6 us
    ppermute x8, waiting for transfers between devices, swap_chan(): lax.ppermute(x, ('frames', 'chan'), self.pairs(lambda f, z: (f, z ^ bit)))  26.4 us
    pallas_call x4, Pallas kernels, fields_back(): pl.pallas_call(fields_back_kernel, grid_spec=pltpu.PrefetchScalarGridSpec...  25 us
  transfers between devices with their start and end apart: 48, of which 18 were waited for; matrix products, arithmetic and copies ran while one was open for 33% of the time, Pallas kernels for 7%

profile of v1, /device:TPU:0, one launch (start us, length us, event | category | flops | bytes accessed | tf_op | source)
XLA Modules:
  0.0 569.2 jit_solution(12361140375651621114)
XLA Ops:
  0.7 6.6 %fusion.30 = bf16[384,768]{1,0:T(8,128)(2,1)} fusion(bf16[3456,768]{1,0:T(8,128)(2,1)} %bitcast.240, bf16[3456,1536]{1,0:T(8,128)(2,1)} %bitcast.248, s32[]{:T(128)S(6)} %select_n.257), kind=kOutput, calls=%fused_computation.54 | convolution fusion | flops 2038726656 | bytes 8552452 | tf_op jit(solution)/shard_map/dot_general | solution.py:22
  7.7 6.5 %fusion.33 = bf16[384,768]{1,0:T(8,128)(2,1)} fusion(bf16[3456,768]{1,0:T(8,128)(2,1)} %bitcast.241, bf16[3456,1536]{1,0:T(8,128)(2,1)} %bitcast.249, s32[]{:T(128)S(6)} %select_n.258), kind=kOutput, calls=%fused_computation.55 | convolution fusion | flops 2038726656 | bytes 8552452 | tf_op jit(solution)/shard_map/dot_general | solution.py:22
  14.2 2.6 collective-permute-start.2
  16.8 6.5 %fusion.36 = bf16[384,768]{1,0:T(8,128)(2,1)} fusion(bf16[3456,768]{1,0:T(8,128)(2,1)} %bitcast.242, bf16[3456,1536]{1,0:T(8,128)(2,1)} %bitcast.250, s32[]{:T(128)S(6)} %select_n.259), kind=kOutput, calls=%fused_computation.56 | convolution fusion | flops 2038726656 | bytes 8552452 | tf_op jit(solution)/shard_map/dot_general | solution.py:22
  23.2 4.3 collective-permute-start.3
  28.4 5.8 %fusion.39 = bf16[384,768]{1,0:T(8,128)(2,1)S(1)} fusion(bf16[3456,768]{1,0:T(8,128)(2,1)} %bitcast.243, bf16[3456,1536]{1,0:T(8,128)(2,1)} %bitcast.251, s32[]{:T(128)S(6)} %select_n.256, bf16[384,768]{1,0:T(8,128)(2,1)} %param.22, f32[768]{0:T(1024)S(1)} %convolution_reduce_fusion), kind=kOutput, calls=%fused_computation.57 | convolution fusion | flops 2039611392 | bytes 9145348 | tf_op jit(solution)/shard_map/dot_general | solution.py:22
  35.1 6.4 %collective-permute-done.2 = bf16[384,768]{1,0:T(8,128)(2,1)S(1)} collective-permute-done((bf16[384,768]{1,0:T(8,128)(2,1)}, bf16[384,768]{1,0:T(8,128)(2,1)S(1)}, u32[]{:S(2)}, u32[]{:S(2)}) %collective-permute-start.2) | collective-permute-done | bytes 589856 | tf_op jit(solution)/shard_map/ppermute | solution.py:48
  41.5 5.0 collective-permute-done.3
  48.2 17.7 %collective-permute-start.5 = (bf16[384,768]{1,0:T(8,128)(2,1)S(1)}, bf16[384,768]{1,0:T(8,128)(2,1)}, u32[]{:S(2)}, u32[]{:S(2)}) collective-permute-start(bf16[384,768]{1,0:T(8,128)(2,1)S(1)} %add_convert_fusion.9), channel_id=1, source_target_pairs={{0,1},{1,0},{2,3},{3,2},{4,5},{5,4},{6,7},{7,6},{8,9},{9,8},{10,11... | collective-permute-start | bytes 1769480 | tf_op jit(solution)/shard_map/ppermute | solution.py:42
  66.0 12.7 %collective-permute-done.5 = bf16[384,768]{1,0:T(8,128)(2,1)} collective-permute-done((bf16[384,768]{1,0:T(8,128)(2,1)S(1)}, bf16[384,768]{1,0:T(8,128)(2,1)}, u32[]{:S(2)}, u32[]{:S(2)}) %collective-permute-start.5) | collective-permute-done | bytes 589856 | tf_op jit(solution)/shard_map/ppermute | solution.py:42
  83.6 8.4 %convolution_convert_fusion.k_ref.v_ref = bf16[1536,1536]{1,0:T(8,128)(2,1)} fusion(bf16[768,2304]{1,0:T(8,128)(2,1)} %param.26, bf16[384,768]{1,0:T(8,128)(2,1)} %collective-permute-done.6, bf16[384,768]{1,0:T(8,128)(2,1)} %collective-permute-done.5, bf16[384,768]{1,0:T(8,128)(2,1)} %collective-permute-done.4, bf16[384,768]{1,0:T(8,128)(2,1)S(1)} %add_convert_fusion.9), kind=kOutput, calls=%fused_computation | convolution fusion | flops 3635675136 | bytes 9437184 | tf_op jit(solution)/shard_map/dot_general | solution.py:22
  92.0 18.3 %attend.1 = (bf16[384,768]{1,0:T(8,128)(2,1)S(1)}, bf16[12,384,1536]{2,1,0:T(8,128)(2,1)}, f32[384,768]{1,0:T(8,128)S(1)}) custom-call(bf16[384,768]{1,0:T(8,128)(2,1)S(1)} %convolution_convert_fusion.8.q_ref, bf16[1536,1536]{1,0:T(8,128)(2,1)} %convolution_convert_fusion.k_ref.v_ref, bf16[1536,1536]{1,0:T(8,128)(2,1)} %convolution_convert_fusion.k_ref.v_ref), custom_call_target="tpu_custom_call" | custom-call | flops 7247757312 | bytes 25165824 | tf_op jit(solution)/shard_map/attend/pallas_call | solution.py:82
  111.8 7.9 %multiply_convert_fusion = (bf16[384,3072]{1,0:T(8,128)(2,1)S(1)}, f32[384,3072]{1,0:T(8,128)}) fusion(f32[3072]{0:T(1024)S(1)} %copy-done.100, bf16[384,768]{1,0:T(8,128)(2,1)S(1)} %add_convert_fusion.8, bf16[768,3072]{1,0:T(8,128)(2,1)} %param.31), kind=kOutput, calls=%fused_computation.14 | convolution fusion | flops 1823735808 | bytes 12398592 | tf_op jit(solution)/shard_map/dot_general | solution.py:22
  122.9 2.8 collective-permute-start.10
  128.5 3.6 collective-permute-start.7
  132.1 6.8 %reshape.309 = bf16[384,4,2,384]{3,2,1,0:T(2,128)(2,1)} reshape(bf16[384,3072]{1,0:T(8,128)(2,1)} %copy-done.53) | data formatting | bytes 4718592 | tf_op jit(solution)/shard_map/reshape | solution.py:335
  141.1 3.2 pad_maximum_fusion.1
  144.2 4.3 copy.114
  148.5 9.6 %constant_dynamic-slice_fusion.2 = (bf16[384,4,1,384]{3,2,1,0:T(2,128)(2,1)}, bf16[384,4,1,384]{3,2,1,0:T(2,128)(2,1)}) fusion(bf16[384,4,2,384]{3,2,1,0:T(2,128)(2,1)} %reshape.309, s32[]{:T(128)S(6)} %select_n.277, s32[]{:T(128)S(6)} %select_n.278), kind=kLoop, calls=%fused_computation.161 | loop fusion | bytes 4718600 | tf_op jit(solution)/shard_map/jit(dynamic_index_in_dim)/dynamic_slice | solution.py:306
  164.0 6.4 %copy.132 = bf16[384,4,1,384]{0,3,1,2:T(8,128)(2,1)} copy(bf16[384,4,1,384]{3,2,1,0:T(2,128)(2,1)} %get-tuple-element.135) | data formatting | bytes 2359296
  170.5 6.5 %copy.131 = bf16[384,4,1,384]{0,3,1,2:T(8,128)(2,1)} copy(bf16[384,4,1,384]{3,2,1,0:T(2,128)(2,1)} %get-tuple-element.134) | data formatting | bytes 2359296
  181.3 4.8 blend.4
  186.1 4.7 blend.5
  191.6 4.6 blend.6
  196.9 14.4 %blend.7 = (bf16[18,64,1536]{2,1,0:T(8,128)(2,1)}, f32[192,384]{1,0:T(8,128)S(1)}, bf16[192,384]{1,0:T(8,128)(2,1)}, f32[3,18,64,1]{3,2,1,0:T(8,128)S(1)}) custom-call(s32[1]{0:T(128)} %bitcast.chunk_ref, bf16[192,384]{1,0:T(8,128)(2,1)} %collective-permute-done.7.logit_ref, bf16[3,18,64,1536]{3,2,1,0:T(8,128)(2,1)} %bitcast.255, ...), custom_call_target="tpu_custom_call", output_to_operand_aliasing={{0}: (5, {})} | custom-call | flops 8388608 | bytes 6291456 | tf_op jit(solution)/shard_map/blend/pallas_call | solution.py:216
  214.1 3.8 collective-permute-start.12
  217.9 2.8 collective-permute-start.11
  224.5 2.5 collective-permute-done.13
  228.5 9.0 %fusion.105 = (bf16[3072]{0:T(1024)(128)(2,1)}, bf16[384,3072]{1,0:T(8,128)(2,1)S(1)}) fusion(f32[384,3072]{1,0:T(8,128)} %get-tuple-element.166, bf16[3072,768]{1,0:T(8,128)(2,1)} %param.33, f32[384,768]{1,0:T(8,128)S(1)} %fusion.106), kind=kOutput, calls=%fused_computation.223 | convolution fusion | flops 1837003776 | bytes 12982272 | tf_op jit(solution)/shard_map/dot_general | solution.py:22
  237.5 5.6 multiply_reduce_fusion
  245.5 19.9 %attend_back.1 = (bf16[384,768]{1,0:T(8,128)(2,1)S(1)}, bf16[1536,768]{1,0:T(8,128)(2,1)S(1)}, bf16[1536,768]{1,0:T(8,128)(2,1)}) custom-call(bf16[384,768]{1,0:T(8,128)(2,1)S(1)} %copy-done.23, bf16[1536,1536]{1,0:T(8,128)(2,1)} %convolution_convert_fusion.k_ref.v_ref, bf16[1536,1536]{1,0:T(8,128)(2,1)} %convolution_convert_fusion.k_ref.v_ref, ...), custom_call_target="tpu_custom_call" | custom-call | flops 18119393280 | bytes 33554432 | tf_op jit(solution)/shard_map/attend_back/pallas_call | solution.py:130
  269.1 5.8 %fusion.104 = (bf16[1536,768]{1,0:T(8,128)(2,1)S(1)}, f32[1536,768]{1,0:T(8,128)}) fusion(bf16[1536,1536]{1,0:T(8,128)(2,1)S(1)} %constant_dynamic-update-slice_fusion, bf16[768,2304]{1,0:T(8,128)(2,1)S(1)} %copy-done.83), kind=kOutput, calls=%fused_computation.222 | convolution fusion | flops 3625058304 | bytes 14155776 | tf_op jit(solution)/shard_map/dot_general | solution.py:22
  279.6 4.2 convolution_convert_fusion.3
  289.3 5.5 convolution_convert_fusion.4
  294.8 2.8 convolution_convert_fusion.2
  300.9 3.8 collective-permute-start.17
  311.4 7.1 %collective-permute-done.17 = bf16[384,768]{1,0:T(8,128)(2,1)} collective-permute-done((bf16[384,768]{1,0:T(8,128)(2,1)}, bf16[384,768]{1,0:T(8,128)(2,1)}, u32[]{:S(2)}, u32[]{:S(2)}) %collective-permute-start.17) | collective-permute-done | bytes 589856 | tf_op jit(solution)/shard_map/ppermute | solution.py:42
  320.5 4.3 add_convert_fusion.3
  328.1 3.6 collective-permute-start.18
  333.8 3.8 collective-permute-done.30
  341.9 7.1 %collective-permute-done.32 = bf16[2,96,1152]{2,1,0:T(8,128)(2,1)S(1)} collective-permute-done((bf16[2,96,1152]{2,1,0:T(8,128)(2,1)S(1)}, bf16[2,96,1152]{2,1,0:T(8,128)(2,1)S(1)}, u32[]{:S(2)}, u32[]{:S(2)}) %collective-permute-start.32) | collective-permute-done | bytes 442400 | tf_op jit(solution)/shard_map/ppermute | solution.py:39
  350.6 5.1 collective-permute-done.18.start_ref
  355.8 3.4 collective-permute-done.19.start_ref
  360.6 11.4 %collective-permute-done.20.start_ref = bf16[400,768]{1,0:T(8,128)(2,1)S(1)} collective-permute-done((bf16[400,768]{1,0:T(8,128)(2,1)S(1)}, bf16[400,768]{1,0:T(8,128)(2,1)S(1)}, u32[]{:S(2)}, u32[]{:S(2)}) %collective-permute-start.20) | collective-permute-done | bytes 614432 | tf_op jit(solution)/shard_map/ppermute | solution.py:54
  375.6 4.3 copy.105
  379.9 2.8 constant_dynamic-slice_fusion.15
  382.7 12.3 %convolution_convert_fusion.1 = bf16[384,3456]{1,0:T(8,128)(2,1)} fusion(bf16[1536,384]{0,1:T(8,128)(2,1)S(1)} %bitcast.298, bf16[3456,1536]{1,0:T(8,128)(2,1)} %bitcast.256), kind=kOutput, calls=%fused_computation.3 | convolution fusion | flops 4078190592 | bytes 14450688 | tf_op jit(solution)/shard_map/dot_general | solution.py:22
  395.1 13.6 %collective-permute-start.22 = (bf16[384,3456]{1,0:T(8,128)(2,1)}, bf16[384,3456]{1,0:T(8,128)(2,1)}, u32[]{:S(2)}, u32[]{:S(2)}) collective-permute-start(bf16[384,3456]{1,0:T(8,128)(2,1)} %convolution_convert_fusion.1), channel_id=1, source_target_pairs={{0,4},{1,5},{2,6},{3,7},{4,0},{5,1},{6,2},{7,3},{8,12},{9,13},{10,... | collective-permute-start | bytes 7962632 | tf_op jit(solution)/shard_map/ppermute | solution.py:39
  409.8 2.7 copy.134
  414.6 2.5 copy-done.5
  417.1 6.2 %fields_back.4.rest_0_ = bf16[3,1152,1536]{2,1,0:T(8,128)(2,1)} custom-call(s32[1]{0:T(128)} %bitcast.11.chunk_ref, bf16[3,1152,768]{2,1,0:T(8,128)(2,1)S(1)} %bitcast.244, bf16[400,768]{1,0:T(8,128)(2,1)S(1)} %copy-done.13, f32[192,384]{1,0:T(8,128)S(1)} %copy-done.21, bf16[18,64,1536]{2,1,0:T(8,128)(2,1)S(1)} %bitcast.236), custom_call_target="tpu_custom_call" | custom-call | flops 2038431744 | bytes 10485760 | tf_op jit(solution)/shard_map/fields_back/pallas_call | solution.py:269
  426.3 6.3 %fields_back.5.rest_0_ = bf16[3,1152,1536]{2,1,0:T(8,128)(2,1)} custom-call(s32[1]{0:T(128)} %bitcast.10.chunk_ref, bf16[3,1152,768]{2,1,0:T(8,128)(2,1)S(1)} %bitcast.245, bf16[400,768]{1,0:T(8,128)(2,1)S(1)} %copy-done.11, f32[192,384]{1,0:T(8,128)S(1)} %copy-done.17, bf16[18,64,1536]{2,1,0:T(8,128)(2,1)S(1)} %bitcast.237, ...), custom_call_target="tpu_custom_call", output_to_operand_aliasing={{}: (5, {})} | custom-call | flops 2038431744 | bytes 10485760 | tf_op jit(solution)/shard_map/fields_back/pallas_call | solution.py:269
  432.6 6.3 %fields_back.6.rest_0_ = bf16[3,1152,1536]{2,1,0:T(8,128)(2,1)} custom-call(s32[1]{0:T(128)} %bitcast.9.chunk_ref, bf16[3,1152,768]{2,1,0:T(8,128)(2,1)S(1)} %bitcast.246, bf16[400,768]{1,0:T(8,128)(2,1)S(1)} %copy-done.9, f32[192,384]{1,0:T(8,128)S(1)} %copy-done.19, bf16[18,64,1536]{2,1,0:T(8,128)(2,1)S(1)} %bitcast.238, ...), custom_call_target="tpu_custom_call", output_to_operand_aliasing={{}: (5, {})} | custom-call | flops 2038431744 | bytes 10485760 | tf_op jit(solution)/shard_map/fields_back/pallas_call | solution.py:269
  438.9 3.1 add_convert_fusion.1
  445.0 3.2 add_convert_fusion.2
  453.5 6.3 %fields_back.7 = bf16[3,1152,1536]{2,1,0:T(8,128)(2,1)} custom-call(s32[1]{0:T(128)} %bitcast.chunk_ref, bf16[3,1152,768]{2,1,0:T(8,128)(2,1)S(1)} %bitcast.247, bf16[400,768]{1,0:T(8,128)(2,1)S(1)} %copy-done.7, f32[192,384]{1,0:T(8,128)S(1)} %copy-done.15, bf16[18,64,1536]{2,1,0:T(8,128)(2,1)S(1)} %bitcast.239, ...), custom_call_target="tpu_custom_call", output_to_operand_aliasing={{}: (5, {})} | custom-call | flops 2038431744 | bytes 10485760 | tf_op jit(solution)/shard_map/fields_back/pallas_call | solution.py:269
  461.7 9.8 %collective-permute-done.44 = bf16[2,384,768]{2,1,0:T(8,128)(2,1)} collective-permute-done((bf16[2,384,768]{2,1,0:T(8,128)(2,1)}, bf16[2,384,768]{2,1,0:T(8,128)(2,1)}, u32[]{:S(2)}, u32[]{:S(2)}) %collective-permute-start.44) | collective-permute-done | bytes 1179680 | tf_op jit(solution)/shard_map/ppermute | solution.py:39
  474.7 12.6 %collective-permute-done.39 = bf16[2,96,4032]{2,1,0:T(8,128)(2,1)S(1)} collective-permute-done((bf16[2,96,4032]{2,1,0:T(8,128)(2,1)}, bf16[2,96,4032]{2,1,0:T(8,128)(2,1)S(1)}, u32[]{:S(2)}, u32[]{:S(2)}) %collective-permute-start.39) | collective-permute-done | bytes 1548320 | tf_op jit(solution)/shard_map/ppermute | solution.py:39
  487.9 11.3 %collective-permute-done.45 = bf16[384,768]{1,0:T(8,128)(2,1)S(1)} collective-permute-done((bf16[384,768]{1,0:T(8,128)(2,1)S(1)}, bf16[384,768]{1,0:T(8,128)(2,1)S(1)}, u32[]{:S(2)}, u32[]{:S(2)}) %collective-permute-start.45) | collective-permute-done | bytes 589856 | tf_op jit(solution)/shard_map/ppermute | solution.py:39
  502.3 5.4 collective-permute-done.46
  510.4 7.7 %add_convert_fusion = bf16[384,3456]{1,0:T(8,128)(2,1)} fusion(bf16[384,3456]{1,0:T(8,128)(2,1)} %collective-permute-done.22, bf16[1536,384]{0,1:T(8,128)(2,1)} %bitcast.296, bf16[3456,1536]{1,0:T(8,128)(2,1)S(1)} %bitcast.259), kind=kOutput, calls=%fused_computation.4 | convolution fusion | flops 4080844800 | bytes 17104896 | tf_op jit(solution)/shard_map/dot_general | solution.py:22
  542.4 6.4 %collective-permute-done.26 = bf16[2,96,2048]{2,1,0:T(8,128)(2,1)} collective-permute-done((bf16[2,96,2048]{2,1,0:T(8,128)(2,1)}, bf16[2,96,2048]{2,1,0:T(8,128)(2,1)}, u32[]{:S(2)}, u32[]{:S(2)}) %collective-permute-start.26) | collective-permute-done | bytes 786464 | tf_op jit(solution)/shard_map/ppermute | solution.py:39
  556.6 3.4 collective-permute-done.27
  566.2 2.8 slice.167
  (416 shorter events, 145.3 us)
Async XLA Ops:
  0.7 109.7 %copy-start = (bf16[768,768]{1,0:T(8,128)(2,1)S(1)}, bf16[768,768]{1,0:T(8,128)(2,1)}, u32[]{:S(2)}) copy-start(bf16[768,768]{1,0:T(8,128)(2,1)} %param.27) | copy-start | bytes 3538948
  7.2 27.9 %collective-permute-start.1 = (bf16[384,768]{1,0:T(8,128)(2,1)}, bf16[384,768]{1,0:T(8,128)(2,1)S(1)}, u32[]{:S(2)}, u32[]{:S(2)}) collective-permute-start(bf16[384,768]{1,0:T(8,128)(2,1)} %fusion.30), channel_id=1, source_target_pairs={{0,4},{1,0},{2,5},{3,1},{4,6},{5,2},{6,7},{7,3},{8,12},{9,8},{10,1... | collective-permute-start | bytes 1769480 | tf_op jit(solution)/shard_map/ppermute | solution.py:48
  14.2 27.4 %collective-permute-start.2 = (bf16[384,768]{1,0:T(8,128)(2,1)}, bf16[384,768]{1,0:T(8,128)(2,1)S(1)}, u32[]{:S(2)}, u32[]{:S(2)}) collective-permute-start(bf16[384,768]{1,0:T(8,128)(2,1)} %fusion.33), channel_id=1, source_target_pairs={{0,1},{1,5},{2,0},{3,4},{4,3},{5,7},{6,2},{7,6},{8,9},{9,13},{10,8... | collective-permute-start | bytes 1769480 | tf_op jit(solution)/shard_map/ppermute | solution.py:48
  23.2 23.3 %collective-permute-start.3 = (bf16[384,768]{1,0:T(8,128)(2,1)}, bf16[384,768]{1,0:T(8,128)(2,1)S(1)}, u32[]{:S(2)}, u32[]{:S(2)}) collective-permute-start(bf16[384,768]{1,0:T(8,128)(2,1)} %fusion.36), channel_id=1, source_target_pairs={{0,5},{1,1},{2,4},{3,0},{4,7},{5,3},{6,6},{7,2},{8,13},{9,9},{10,1... | collective-permute-start | bytes 1769480 | tf_op jit(solution)/shard_map/ppermute | solution.py:48
  34.2 12.3 %collective-permute-start = (bf16[384,768]{1,0:T(8,128)(2,1)S(1)}, bf16[384,768]{1,0:T(8,128)(2,1)S(1)}, u32[]{:S(2)}, u32[]{:S(2)}) collective-permute-start(bf16[384,768]{1,0:T(8,128)(2,1)S(1)} %fusion.39), channel_id=1, source_target_pairs={{0,0},{1,4},{2,1},{3,5},{4,2},{5,6},{6,3},{7,7},{8,8},{9,12},{10,9... | collective-permute-start | bytes 1769480 | tf_op jit(solution)/shard_map/ppermute | solution.py:48
  48.2 35.4 %copy-start.46 = (bf16[384,768]{1,0:T(8,128)(2,1)}, bf16[384,768]{1,0:T(8,128)(2,1)S(1)}, u32[]{:S(2)}) copy-start(bf16[384,768]{1,0:T(8,128)(2,1)S(1)} %add_convert_fusion.9) | copy-start | bytes 1769476
  48.2 30.4 %collective-permute-start.5 = (bf16[384,768]{1,0:T(8,128)(2,1)S(1)}, bf16[384,768]{1,0:T(8,128)(2,1)}, u32[]{:S(2)}, u32[]{:S(2)}) collective-permute-start(bf16[384,768]{1,0:T(8,128)(2,1)S(1)} %add_convert_fusion.9), channel_id=1, source_target_pairs={{0,1},{1,0},{2,3},{3,2},{4,5},{5,4},{6,7},{7,6},{8,9},{9,8},{10,11... | collective-permute-start | bytes 1769480 | tf_op jit(solution)/shard_map/ppermute | solution.py:42
  66.0 17.6 %collective-permute-start.4 = (bf16[384,768]{1,0:T(8,128)(2,1)S(1)}, bf16[384,768]{1,0:T(8,128)(2,1)}, u32[]{:S(2)}, u32[]{:S(2)}) collective-permute-start(bf16[384,768]{1,0:T(8,128)(2,1)S(1)} %add_convert_fusion.9), channel_id=1, source_target_pairs={{0,4},{1,5},{2,6},{3,7},{4,0},{5,1},{6,2},{7,3},{8,12},{9,13},{10,... | collective-permute-start | bytes 1769480 | tf_op jit(solution)/shard_map/ppermute | solution.py:39
  78.6 4.9 collective-permute-start.6
  92.0 18.3 %copy-start.27 = (f32[384,768]{1,0:T(8,128)S(1)}, f32[384,768]{1,0:T(8,128)}, u32[]{:S(2)}) copy-start(f32[384,768]{1,0:T(8,128)} %copy-done.26) | copy-start | bytes 3538948
  92.0 18.3 %copy-start.98 = (f32[768]{0:T(1024)S(1)}, f32[768]{0:T(1024)}, u32[]{:S(2)}) copy-start(f32[768]{0:T(1024)} %param.28) | copy-start | bytes 9220
  122.9 56.4 %collective-permute-start.10 = (bf16[192,384]{1,0:T(8,128)(2,1)}, bf16[192,384]{1,0:T(8,128)(2,1)}, u32[]{:S(2)}, u32[]{:S(2)}) collective-permute-start(bf16[192,384]{1,0:T(8,128)(2,1)} %fusion.47), channel_id=1, source_target_pairs={{0,0},{4,1},{1,2},{5,3},{2,4},{6,5},{3,6},{7,7},{8,8},{12,9},{9,10... | collective-permute-start | bytes 442376 | tf_op jit(solution)/shard_map/ppermute | solution.py:54
  125.7 60.4 %collective-permute-start.9 = (bf16[192,384]{1,0:T(8,128)(2,1)}, bf16[192,384]{1,0:T(8,128)(2,1)}, u32[]{:S(2)}, u32[]{:S(2)}) collective-permute-start(bf16[192,384]{1,0:T(8,128)(2,1)} %fusion.47), channel_id=1, source_target_pairs={{4,0},{0,1},{5,2},{1,3},{6,4},{2,5},{7,6},{3,7},{12,8},{8,9},{13,1... | collective-permute-start | bytes 442376 | tf_op jit(solution)/shard_map/ppermute | solution.py:54
  127.8 63.7 %collective-permute-start.8 = (bf16[192,384]{1,0:T(8,128)(2,1)}, bf16[192,384]{1,0:T(8,128)(2,1)}, u32[]{:S(2)}, u32[]{:S(2)}) collective-permute-start(bf16[192,384]{1,0:T(8,128)(2,1)} %fusion.47), channel_id=1, source_target_pairs={{1,0},{5,1},{0,2},{4,3},{3,4},{7,5},{2,6},{6,7},{9,8},{13,9},{8,10... | collective-permute-start | bytes 442376 | tf_op jit(solution)/shard_map/ppermute | solution.py:54
  128.5 68.5 %collective-permute-start.7 = (bf16[192,384]{1,0:T(8,128)(2,1)}, bf16[192,384]{1,0:T(8,128)(2,1)}, u32[]{:S(2)}, u32[]{:S(2)}) collective-permute-start(bf16[192,384]{1,0:T(8,128)(2,1)} %fusion.47), channel_id=1, source_target_pairs={{5,0},{1,1},{4,2},{0,3},{7,4},{3,5},{6,6},{2,7},{13,8},{9,9},{12,1... | collective-permute-start | bytes 442376 | tf_op jit(solution)/shard_map/ppermute | solution.py:54
  212.0 12.5 %collective-permute-start.14 = (bf16[192,384]{1,0:T(8,128)(2,1)}, bf16[192,384]{1,0:T(8,128)(2,1)S(1)}, u32[]{:S(2)}, u32[]{:S(2)}) collective-permute-start(bf16[192,384]{1,0:T(8,128)(2,1)} %get-tuple-element.48), channel_id=1, source_target_pairs={{0,5},{1,1},{2,4},{3,0},{4,7},{5,3},{6,6},{7,2},{8,13},{9,9},{10,1... | collective-permute-start | bytes 442376 | tf_op jit(solution)/shard_map/ppermute | solution.py:48
  213.9 13.0 %collective-permute-start.13 = (bf16[192,384]{1,0:T(8,128)(2,1)}, bf16[192,384]{1,0:T(8,128)(2,1)S(1)}, u32[]{:S(2)}, u32[]{:S(2)}) collective-permute-start(bf16[192,384]{1,0:T(8,128)(2,1)} %get-tuple-element.47), channel_id=1, source_target_pairs={{0,1},{1,5},{2,0},{3,4},{4,3},{5,7},{6,2},{7,6},{8,9},{9,13},{10,8... | collective-permute-start | bytes 442376 | tf_op jit(solution)/shard_map/ppermute | solution.py:48
  214.1 12.8 %collective-permute-start.12 = (bf16[192,384]{1,0:T(8,128)(2,1)}, bf16[192,384]{1,0:T(8,128)(2,1)}, u32[]{:S(2)}, u32[]{:S(2)}) collective-permute-start(bf16[192,384]{1,0:T(8,128)(2,1)} %get-tuple-element.46), channel_id=1, source_target_pairs={{0,4},{1,0},{2,5},{3,1},{4,6},{5,2},{6,7},{7,3},{8,12},{9,8},{10,1... | collective-permute-start | bytes 442376 | tf_op jit(solution)/shard_map/ppermute | solution.py:48
  217.9 9.0 %collective-permute-start.11 = (bf16[192,384]{1,0:T(8,128)(2,1)}, bf16[192,384]{1,0:T(8,128)(2,1)}, u32[]{:S(2)}, u32[]{:S(2)}) collective-permute-start(bf16[192,384]{1,0:T(8,128)(2,1)} %get-tuple-element.45), channel_id=1, source_target_pairs={{0,0},{1,4},{2,1},{3,5},{4,2},{5,6},{6,3},{7,7},{8,8},{9,12},{10,9... | collective-permute-start | bytes 442376 | tf_op jit(solution)/shard_map/ppermute | solution.py:48
  276.1 21.7 %collective-permute-start.16 = (bf16[384,768]{1,0:T(8,128)(2,1)}, bf16[384,768]{1,0:T(8,128)(2,1)}, u32[]{:S(2)}, u32[]{:S(2)}) collective-permute-start(bf16[384,768]{1,0:T(8,128)(2,1)} %get-tuple-element.141), channel_id=1, source_target_pairs={{0,4},{1,5},{2,6},{3,7},{4,0},{5,1},{6,2},{7,3},{8,12},{9,13},{10,... | collective-permute-start | bytes 1769480 | tf_op jit(solution)/shard_map/ppermute | solution.py:39
  276.1 35.3 %collective-permute-start.15 = (bf16[384,768]{1,0:T(8,128)(2,1)}, bf16[384,768]{1,0:T(8,128)(2,1)}, u32[]{:S(2)}, u32[]{:S(2)}) collective-permute-start(bf16[384,768]{1,0:T(8,128)(2,1)} %get-tuple-element.140), channel_id=1, source_target_pairs={{0,4},{1,5},{2,6},{3,7},{4,0},{5,1},{6,2},{7,3},{8,12},{9,13},{10,... | collective-permute-start | bytes 1769480 | tf_op jit(solution)/shard_map/ppermute | solution.py:39
  283.7 155.2 %collective-permute-start.43 = (bf16[1536,768]{1,0:T(8,128)(2,1)}, bf16[1536,768]{1,0:T(8,128)(2,1)}, u32[]{:S(2)}, u32[]{:S(2)}) collective-permute-start(bf16[1536,768]{1,0:T(8,128)(2,1)} %convolution_convert_fusion.3), channel_id=1, source_target_pairs={{0,4},{1,5},{2,6},{3,7},{4,0},{5,1},{6,2},{7,3},{8,12},{9,13},{10,... | collective-permute-start | bytes 7077896 | tf_op jit(solution)/shard_map/ppermute | solution.py:39
  285.0 24.0 %collective-permute-start.37 = (bf16[384,768]{1,0:T(8,128)(2,1)}, bf16[384,768]{1,0:T(8,128)(2,1)}, u32[]{:S(2)}, u32[]{:S(2)}) collective-permute-start(bf16[384,768]{1,0:T(8,128)(2,1)} %convolution_convert_fusion.5), channel_id=1, source_target_pairs={{0,4},{1,5},{2,6},{3,7},{4,0},{5,1},{6,2},{7,3},{8,12},{9,13},{10,... | collective-permute-start | bytes 1769480 | tf_op jit(solution)/shard_map/ppermute | solution.py:39
  289.2 18.1 %collective-permute-start.28 = (bf16[384,768]{1,0:T(8,128)(2,1)}, bf16[384,768]{1,0:T(8,128)(2,1)}, u32[]{:S(2)}, u32[]{:S(2)}) collective-permute-start(bf16[384,768]{1,0:T(8,128)(2,1)} %convolution_convert_fusion.6), channel_id=1, source_target_pairs={{0,4},{1,5},{2,6},{3,7},{4,0},{5,1},{6,2},{7,3},{8,12},{9,13},{10,... | collective-permute-start | bytes 1769480 | tf_op jit(solution)/shard_map/ppermute | solution.py:39
  297.9 3.0 collective-permute-start.38
  300.9 17.6 %collective-permute-start.17 = (bf16[384,768]{1,0:T(8,128)(2,1)}, bf16[384,768]{1,0:T(8,128)(2,1)}, u32[]{:S(2)}, u32[]{:S(2)}) collective-permute-start(bf16[384,768]{1,0:T(8,128)(2,1)} %fusion.44), channel_id=1, source_target_pairs={{0,1},{1,0},{2,3},{3,2},{4,5},{5,4},{6,7},{7,6},{8,9},{9,8},{10,11... | collective-permute-start | bytes 1769480 | tf_op jit(solution)/shard_map/ppermute | solution.py:42
  307.3 13.1 %collective-permute-start.29 = (bf16[384,1536]{1,0:T(8,128)(2,1)}, bf16[384,1536]{1,0:T(8,128)(2,1)S(1)}, u32[]{:S(2)}, u32[]{:S(2)}) collective-permute-start(bf16[384,1536]{1,0:T(8,128)(2,1)} %convolution_convert_fusion.4), channel_id=1, source_target_pairs={{0,4},{1,5},{2,6},{3,7},{4,0},{5,1},{6,2},{7,3},{8,12},{9,13},{10,... | collective-permute-start | bytes 3538952 | tf_op jit(solution)/shard_map/ppermute | solution.py:39
  325.9 11.8 %collective-permute-start.30 = (bf16[2,96,1152]{2,1,0:T(8,128)(2,1)}, bf16[2,96,1152]{2,1,0:T(8,128)(2,1)S(1)}, u32[]{:S(2)}, u32[]{:S(2)}) collective-permute-start(bf16[2,96,1152]{2,1,0:T(8,128)(2,1)} %dynamic-slice_bitcast_fusion.8), channel_id=1, source_target_pairs={{0,8},{1,9},{2,10},{3,11},{4,12},{5,13},{6,14},{7,15},{8,0},{9,1},... | collective-permute-start | bytes 1327112 | tf_op jit(solution)/shard_map/ppermute | solution.py:39
  328.1 27.7 %collective-permute-start.18 = (bf16[400,768]{1,0:T(8,128)(2,1)S(1)}, bf16[400,768]{1,0:T(8,128)(2,1)S(1)}, u32[]{:S(2)}, u32[]{:S(2)}) collective-permute-start(bf16[400,768]{1,0:T(8,128)(2,1)S(1)} %fusion.56), channel_id=1, source_target_pairs={{5,0},{1,1},{4,2},{0,3},{7,4},{3,5},{6,6},{2,7},{13,8},{9,9},{12,1... | collective-permute-start | bytes 1843208 | tf_op jit(solution)/shard_map/ppermute | solution.py:54
  331.7 27.4 %collective-permute-start.19 = (bf16[400,768]{1,0:T(8,128)(2,1)S(1)}, bf16[400,768]{1,0:T(8,128)(2,1)S(1)}, u32[]{:S(2)}, u32[]{:S(2)}) collective-permute-start(bf16[400,768]{1,0:T(8,128)(2,1)S(1)} %fusion.56), channel_id=1, source_target_pairs={{1,0},{5,1},{0,2},{4,3},{3,4},{7,5},{2,6},{6,7},{9,8},{13,9},{8,10... | collective-permute-start | bytes 1843208 | tf_op jit(solution)/shard_map/ppermute | solution.py:54
  332.0 40.0 %collective-permute-start.20 = (bf16[400,768]{1,0:T(8,128)(2,1)S(1)}, bf16[400,768]{1,0:T(8,128)(2,1)S(1)}, u32[]{:S(2)}, u32[]{:S(2)}) collective-permute-start(bf16[400,768]{1,0:T(8,128)(2,1)S(1)} %fusion.56), channel_id=1, source_target_pairs={{4,0},{0,1},{5,2},{1,3},{6,4},{2,5},{7,6},{3,7},{12,8},{8,9},{13,1... | collective-permute-start | bytes 1843208 | tf_op jit(solution)/shard_map/ppermute | solution.py:54
  338.4 10.6 %collective-permute-start.32 = (bf16[2,96,1152]{2,1,0:T(8,128)(2,1)S(1)}, bf16[2,96,1152]{2,1,0:T(8,128)(2,1)S(1)}, u32[]{:S(2)}, u32[]{:S(2)}) collective-permute-start(bf16[2,96,1152]{2,1,0:T(8,128)(2,1)S(1)} %dynamic-slice_bitcast_fusion.7), channel_id=1, source_target_pairs={{0,16},{1,17},{2,18},{3,19},{4,20},{5,21},{6,22},{7,23},{8,24},{9,... | collective-permute-start | bytes 1327112 | tf_op jit(solution)/shard_map/ppermute | solution.py:39
  349.0 23.5 %collective-permute-start.21 = (bf16[400,768]{1,0:T(8,128)(2,1)S(1)}, bf16[400,768]{1,0:T(8,128)(2,1)S(1)}, u32[]{:S(2)}, u32[]{:S(2)}) collective-permute-start(bf16[400,768]{1,0:T(8,128)(2,1)S(1)} %fusion.56), channel_id=1, source_target_pairs={{0,0},{4,1},{1,2},{5,3},{2,4},{6,5},{3,6},{7,7},{8,8},{12,9},{9,10... | collective-permute-start | bytes 1843208 | tf_op jit(solution)/shard_map/ppermute | solution.py:54
  349.9 22.7 %copy-start.63 = (bf16[2,96,1152]{2,1,0:T(8,128)(2,1)}, bf16[2,96,1152]{2,1,0:T(8,128)(2,1)S(1)}, u32[]{:S(2)}) copy-start(bf16[2,96,1152]{2,1,0:T(8,128)(2,1)S(1)} %fusion.51) | copy-start | bytes 1327108
  355.8 53.0 %copy-start.6 = (bf16[400,768]{1,0:T(8,128)(2,1)}, bf16[400,768]{1,0:T(8,128)(2,1)S(1)}, u32[]{:S(2)}) copy-start(bf16[400,768]{1,0:T(8,128)(2,1)S(1)} %collective-permute-done.18.start_ref) | copy-start | bytes 1843204
  355.8 88.0 %collective-permute-start.36 = (bf16[384,3072]{1,0:T(8,128)(2,1)}, bf16[384,3072]{1,0:T(8,128)(2,1)}, u32[]{:S(2)}, u32[]{:S(2)}) collective-permute-start(bf16[384,3072]{1,0:T(8,128)(2,1)} %convolution_convert_fusion.2), channel_id=1, source_target_pairs={{0,4},{1,5},{2,6},{3,7},{4,0},{5,1},{6,2},{7,3},{8,12},{9,13},{10,... | collective-permute-start | bytes 7077896 | tf_op jit(solution)/shard_map/ppermute | solution.py:39
  359.1 49.6 %copy-start.8 = (bf16[400,768]{1,0:T(8,128)(2,1)}, bf16[400,768]{1,0:T(8,128)(2,1)S(1)}, u32[]{:S(2)}) copy-start(bf16[400,768]{1,0:T(8,128)(2,1)S(1)} %collective-permute-done.19.start_ref) | copy-start | bytes 1843204
  359.1 64.2 %collective-permute-start.31 = (bf16[96,1152]{1,0:T(8,128)(2,1)}, bf16[96,1152]{1,0:T(8,128)(2,1)}, u32[]{:S(2)}, u32[]{:S(2)}) collective-permute-start(bf16[96,1152]{1,0:T(8,128)(2,1)} %dynamic-slice_bitcast_fusion.15), channel_id=1, source_target_pairs={{0,16},{1,17},{2,18},{3,19},{4,20},{5,21},{6,22},{7,23},{8,24},{9,... | collective-permute-start | bytes 663560 | tf_op jit(solution)/shard_map/ppermute | solution.py:39
  372.0 36.8 %copy-start.10 = (bf16[400,768]{1,0:T(8,128)(2,1)}, bf16[400,768]{1,0:T(8,128)(2,1)S(1)}, u32[]{:S(2)}) copy-start(bf16[400,768]{1,0:T(8,128)(2,1)S(1)} %collective-permute-done.20.start_ref) | copy-start | bytes 1843204
  372.0 52.5 %collective-permute-start.33 = (bf16[96,1152]{1,0:T(8,128)(2,1)}, bf16[96,1152]{1,0:T(8,128)(2,1)}, u32[]{:S(2)}, u32[]{:S(2)}) collective-permute-start(bf16[96,1152]{1,0:T(8,128)(2,1)} %dynamic-slice_bitcast_fusion.14), channel_id=1, source_target_pairs={{0,8},{1,9},{2,10},{3,11},{4,12},{5,13},{6,14},{7,15},{8,0},{9,1},... | collective-permute-start | bytes 663560 | tf_op jit(solution)/shard_map/ppermute | solution.py:39
  372.5 36.2 %copy-start.12 = (bf16[400,768]{1,0:T(8,128)(2,1)}, bf16[400,768]{1,0:T(8,128)(2,1)S(1)}, u32[]{:S(2)}) copy-start(bf16[400,768]{1,0:T(8,128)(2,1)S(1)} %collective-permute-done.21.start_ref) | copy-start | bytes 1843204
  382.7 25.9 %copy-start.99 = (f32[40]{0:T(128)S(1)}, f32[40]{0:T(128)}, u32[]{:S(2)}) copy-start(f32[40]{0:T(128)} %fusion.76) | copy-start | bytes 484
  382.7 26.1 %copy-start.60 = (bf16[768,384]{0,1:T(8,128)(2,1)S(1)}, bf16[768,384]{0,1:T(8,128)(2,1)}, u32[]{:S(2)}) copy-start(bf16[768,384]{0,1:T(8,128)(2,1)} %get-tuple-element.147) | copy-start | bytes 1769476
  382.7 26.1 %copy-start.84 = (bf16[768,54]{0,1:T(8,128)(2,1)S(1)}, bf16[768,54]{0,1:T(8,128)(2,1)}, u32[]{:S(2)}) copy-start(bf16[768,54]{0,1:T(8,128)(2,1)} %copy.127) | copy-start | bytes 248836
  395.1 115.3 %collective-permute-start.22 = (bf16[384,3456]{1,0:T(8,128)(2,1)}, bf16[384,3456]{1,0:T(8,128)(2,1)}, u32[]{:S(2)}, u32[]{:S(2)}) collective-permute-start(bf16[384,3456]{1,0:T(8,128)(2,1)} %convolution_convert_fusion.1), channel_id=1, source_target_pairs={{0,4},{1,5},{2,6},{3,7},{4,0},{5,1},{6,2},{7,3},{8,12},{9,13},{10,... | collective-permute-start | bytes 7962632 | tf_op jit(solution)/shard_map/ppermute | solution.py:39
  423.3 37.1 %collective-permute-start.25 = (bf16[4,96,512]{2,1,0:T(8,128)(2,1)}, bf16[4,96,512]{2,1,0:T(8,128)(2,1)}, u32[]{:S(2)}, u32[]{:S(2)}) collective-permute-start(bf16[4,96,512]{2,1,0:T(8,128)(2,1)} %dynamic-slice_bitcast_fusion.10), channel_id=1, source_target_pairs={{0,4},{1,5},{2,6},{3,7},{4,0},{5,1},{6,2},{7,3},{8,12},{9,13},{10,... | collective-permute-start | bytes 1179656 | tf_op jit(solution)/shard_map/ppermute | solution.py:39
  425.5 13.3 %collective-permute-start.34 = (bf16[2,24,2304]{2,1,0:T(8,128)(2,1)S(1)}, bf16[2,24,2304]{2,1,0:T(8,128)(2,1)S(1)}, u32[]{:S(2)}, u32[]{:S(2)}) collective-permute-start(bf16[2,24,2304]{2,1,0:T(8,128)(2,1)S(1)} %dynamic-slice_bitcast_fusion.13), channel_id=1, source_target_pairs={{0,1},{1,0},{2,3},{3,2},{4,5},{5,4},{6,7},{7,6},{8,9},{9,8},{10,11... | collective-permute-start | bytes 663560 | tf_op jit(solution)/shard_map/ppermute | solution.py:42
  443.2 28.3 %collective-permute-start.44 = (bf16[2,384,768]{2,1,0:T(8,128)(2,1)}, bf16[2,384,768]{2,1,0:T(8,128)(2,1)}, u32[]{:S(2)}, u32[]{:S(2)}) collective-permute-start(bf16[2,384,768]{2,1,0:T(8,128)(2,1)} %dynamic-slice_bitcast_fusion.1), channel_id=1, source_target_pairs={{0,8},{1,9},{2,10},{3,11},{4,12},{5,13},{6,14},{7,15},{8,0},{9,1},... | collective-permute-start | bytes 3538952 | tf_op jit(solution)/shard_map/ppermute | solution.py:39
  449.9 37.4 %collective-permute-start.39 = (bf16[2,96,4032]{2,1,0:T(8,128)(2,1)}, bf16[2,96,4032]{2,1,0:T(8,128)(2,1)S(1)}, u32[]{:S(2)}, u32[]{:S(2)}) collective-permute-start(bf16[2,96,4032]{2,1,0:T(8,128)(2,1)} %dynamic-slice_bitcast_fusion), channel_id=1, source_target_pairs={{0,16},{1,17},{2,18},{3,19},{4,20},{5,21},{6,22},{7,23},{8,24},{9,... | collective-permute-start | bytes 4644872 | tf_op jit(solution)/shard_map/ppermute | solution.py:39
  451.4 8.4 %collective-permute-start.35 = (bf16[24,2304]{1,0:T(8,128)(2,1)S(1)}, bf16[24,2304]{1,0:T(8,128)(2,1)S(1)}, u32[]{:S(2)}, u32[]{:S(2)}) collective-permute-start(bf16[24,2304]{1,0:T(8,128)(2,1)S(1)} %dynamic-slice_bitcast_fusion.18), channel_id=1, source_target_pairs={{0,2},{1,3},{2,0},{3,1},{4,6},{5,7},{6,4},{7,5},{8,10},{9,11},{10,... | collective-permute-start | bytes 331784 | tf_op jit(solution)/shard_map/ppermute | solution.py:42
  453.4 57.0 %slice-start = ((s8[10616832]{0:T(1024)(128)(4,1)}), s8[4194304]{0:T(1024)(128)(4,1)S(1)}, s32[]{:S(2)}) async-start(s8[10616832]{0:T(1024)(128)(4,1)} %bitcast.257), calls=%async_computation | async-start | bytes 8388608
  453.4 56.9 %slice-start.1 = ((s8[10616832]{0:T(1024)(128)(4,1)}), s8[4194304]{0:T(1024)(128)(4,1)S(1)}, s32[]{:S(2)}) async-start(s8[10616832]{0:T(1024)(128)(4,1)} %bitcast.257), calls=%async_computation.1 | async-start | bytes 8388608
  460.4 50.0 %slice-start.2 = ((s8[10616832]{0:T(1024)(128)(4,1)}), s8[2228224]{0:T(1024)(128)(4,1)S(1)}, s32[]{:S(2)}) async-start(s8[10616832]{0:T(1024)(128)(4,1)} %bitcast.257), calls=%async_computation.2 | async-start | bytes 4456448
  461.7 25.6 %copy-start.34 = (bf16[2,2,96,4032]{3,2,1,0:T(8,128)(2,1)S(1)}, bf16[2,2,96,4032]{3,2,1,0:T(8,128)(2,1)}, u32[]{:S(2)}) copy-start(bf16[2,2,96,4032]{3,2,1,0:T(8,128)(2,1)} %copy-done.33) | copy-start | bytes 9289732
  473.2 26.0 %collective-permute-start.45 = (bf16[384,768]{1,0:T(8,128)(2,1)S(1)}, bf16[384,768]{1,0:T(8,128)(2,1)S(1)}, u32[]{:S(2)}, u32[]{:S(2)}) collective-permute-start(bf16[384,768]{1,0:T(8,128)(2,1)S(1)} %dynamic-slice_bitcast_fusion.5), channel_id=1, source_target_pairs={{0,16},{1,17},{2,18},{3,19},{4,20},{5,21},{6,22},{7,23},{8,24},{9,... | collective-permute-start | bytes 1769480 | tf_op jit(solution)/shard_map/ppermute | solution.py:39
  499.4 8.3 %collective-permute-start.46 = (bf16[2,96,768]{2,1,0:T(8,128)(2,1)S(1)}, bf16[2,96,768]{2,1,0:T(8,128)(2,1)S(1)}, u32[]{:S(2)}, u32[]{:S(2)}) collective-permute-start(bf16[2,96,768]{2,1,0:T(8,128)(2,1)S(1)} %dynamic-slice_bitcast_fusion.12), channel_id=1, source_target_pairs={{0,1},{1,0},{2,3},{3,2},{4,5},{5,4},{6,7},{7,6},{8,9},{9,8},{10,11... | collective-permute-start | bytes 884744 | tf_op jit(solution)/shard_map/ppermute | solution.py:42
  501.7 21.4 %collective-permute-start.40 = (bf16[96,4032]{1,0:T(8,128)(2,1)}, bf16[96,4032]{1,0:T(8,128)(2,1)}, u32[]{:S(2)}, u32[]{:S(2)}) collective-permute-start(bf16[96,4032]{1,0:T(8,128)(2,1)} %dynamic-slice_bitcast_fusion.2), channel_id=1, source_target_pairs={{0,8},{1,9},{2,10},{3,11},{4,12},{5,13},{6,14},{7,15},{8,0},{9,1},... | collective-permute-start | bytes 2322440 | tf_op jit(solution)/shard_map/ppermute | solution.py:39
  509.1 21.9 %collective-permute-start.47 = (bf16[96,768]{1,0:T(8,128)(2,1)}, bf16[96,768]{1,0:T(8,128)(2,1)}, u32[]{:S(2)}, u32[]{:S(2)}) collective-permute-start(bf16[96,768]{1,0:T(8,128)(2,1)} %dynamic-slice_bitcast_fusion.17), channel_id=1, source_target_pairs={{0,2},{1,3},{2,0},{3,1},{4,6},{5,7},{6,4},{7,5},{8,10},{9,11},{10,... | collective-permute-start | bytes 442376 | tf_op jit(solution)/shard_map/ppermute | solution.py:42
  522.4 16.4 %collective-permute-start.23 = (bf16[2,96,1920]{2,1,0:T(8,128)(2,1)}, bf16[2,96,1920]{2,1,0:T(8,128)(2,1)}, u32[]{:S(2)}, u32[]{:S(2)}) collective-permute-start(bf16[2,96,1920]{2,1,0:T(8,128)(2,1)} %dynamic-slice_bitcast_fusion.4), channel_id=1, source_target_pairs={{0,8},{1,9},{2,10},{3,11},{4,12},{5,13},{6,14},{7,15},{8,0},{9,1},... | collective-permute-start | bytes 2211848 | tf_op jit(solution)/shard_map/ppermute | solution.py:39
  525.2 8.8 %collective-permute-start.41 = (bf16[2,24,4032]{2,1,0:T(8,128)(2,1)}, bf16[2,24,4032]{2,1,0:T(8,128)(2,1)}, u32[]{:S(2)}, u32[]{:S(2)}) collective-permute-start(bf16[2,24,4032]{2,1,0:T(8,128)(2,1)} %dynamic-slice_bitcast_fusion.9), channel_id=1, source_target_pairs={{0,1},{1,0},{2,3},{3,2},{4,5},{5,4},{6,7},{7,6},{8,9},{9,8},{10,11... | collective-permute-start | bytes 1161224 | tf_op jit(solution)/shard_map/ppermute | solution.py:42
  528.0 20.8 %collective-permute-start.26 = (bf16[2,96,2048]{2,1,0:T(8,128)(2,1)}, bf16[2,96,2048]{2,1,0:T(8,128)(2,1)}, u32[]{:S(2)}, u32[]{:S(2)}) collective-permute-start(bf16[2,96,2048]{2,1,0:T(8,128)(2,1)} %get-tuple-element.143), channel_id=1, source_target_pairs={{0,16},{1,17},{2,18},{3,19},{4,20},{5,21},{6,22},{7,23},{8,24},{9,... | collective-permute-start | bytes 2359304 | tf_op jit(solution)/shard_map/ppermute | solution.py:39
  535.2 17.1 %collective-permute-start.42 = (bf16[24,4032]{1,0:T(8,128)(2,1)S(1)}, bf16[24,4032]{1,0:T(8,128)(2,1)}, u32[]{:S(2)}, u32[]{:S(2)}) collective-permute-start(bf16[24,4032]{1,0:T(8,128)(2,1)S(1)} %dynamic-slice_bitcast_fusion.16), channel_id=1, source_target_pairs={{0,2},{1,3},{2,0},{3,1},{4,6},{5,7},{6,4},{7,5},{8,10},{9,11},{10,... | collective-permute-start | bytes 580616 | tf_op jit(solution)/shard_map/ppermute | solution.py:42
  540.9 14.3 %collective-permute-start.24 = (bf16[96,1920]{1,0:T(8,128)(2,1)}, bf16[96,1920]{1,0:T(8,128)(2,1)}, u32[]{:S(2)}, u32[]{:S(2)}) collective-permute-start(bf16[96,1920]{1,0:T(8,128)(2,1)} %dynamic-slice_bitcast_fusion.11), channel_id=1, source_target_pairs={{0,16},{1,17},{2,18},{3,19},{4,20},{5,21},{6,22},{7,23},{8,24},{9,... | collective-permute-start | bytes 1105928 | tf_op jit(solution)/shard_map/ppermute | solution.py:39
  550.7 9.2 %collective-permute-start.27 = (bf16[96,2048]{0,1:T(8,128)(2,1)S(1)}, bf16[96,2048]{0,1:T(8,128)(2,1)S(1)}, u32[]{:S(2)}, u32[]{:S(2)}) collective-permute-start(bf16[96,2048]{0,1:T(8,128)(2,1)S(1)} %dynamic-slice_bitcast_fusion.6), channel_id=1, source_target_pairs={{0,8},{1,9},{2,10},{3,11},{4,12},{5,13},{6,14},{7,15},{8,0},{9,1},... | collective-permute-start | bytes 1179656 | tf_op jit(solution)/shard_map/ppermute | solution.py:39
  (91 other events, 462.6 us)
